TPU v7x, 128 devices: a whole 4x4x4 slice. The times are simulated.
128 devices in a mesh: row: 16 (over y, z), col: 8 (over x, core).
Axes of the slice: x: 4, y: 4, z: 4, core: 2. Of those that a mesh axis runs over, the one named last changes fastest.
Arguments:
- object_real: float32 [8192, 4096], P('row', 'col'), may hold values from -5 to 5
- object_imag: float32 [8192, 4096], P('row', 'col'), may hold values from -5 to 5
- probe_real: float32 [4, 256, 256], replicated, may hold values from -6 to 6
- probe_imag: float32 [4, 256, 256], replicated, may hold values from -6 to 6
- amplitudes: float32 [16, 8, 8, 256, 256], P('row', 'col'), may hold values from 0 to 3
- positions: int32 [16, 8, 8, 2], P('row', 'col'), may hold values from 0 to 511, as said below
- counts: int32 [16, 8], P('row', 'col'), may hold values from 1 to 8, as said below
Outputs:
- new_object_real: float32 [8192, 4096], P('row', 'col')
- new_object_imag: float32 [8192, 4096], P('row', 'col')
- new_probe_real: float32 [4, 256, 256], replicated
- new_probe_imag: float32 [4, 256, 256], replicated
Inputs may be any that keep to these rules, and one draw needn't show every extreme that they name: `positions`: offsets lie within the device's tile; on the last row of devices the row offset is at most 256, on the last column the column offset likewise, so every frame's window lies inside the object. `counts`: slots from the count on hold no frame.
All inputs are finite; a program needn't handle non-finite values.
Results may differ from a plain program's by a relative error of at most 0.0046.
Values sent between devices are 32-bit elements; how exact they have to be, the bound alone decides.
A program may use at most 128 MiB of HBM per device.

v0:
```python
import math

import jax
import jax.numpy as jnp
import numpy as np
from jax import lax
from jax.experimental import pallas as pl
from jax.experimental.pallas import tpu as pltpu
from jax.sharding import PartitionSpec as P

OBJECT_STEP = 0.25
PROBE_STEP = 0.5
MESH = pl.DeviceIdType.MESH
F32 = jnp.float32
BF16 = jnp.bfloat16
LANES = 128
SIZE = 256
MODES = 4
TILE = 512
SPAN = TILE + SIZE
SLOTS = 8
CHUNK = 32
VMEM_LIMIT = 56 * 2**20


def tables():
    index = np.arange(SIZE)
    angle = (index[:, None] * index[None, :] % SIZE) * (2.0 * math.pi / SIZE)
    scale = 1.0 / math.sqrt(SIZE)
    cos_t = (np.cos(angle) * scale).astype(BF16)
    sin_t = (-np.sin(angle) * scale).astype(BF16)
    found = []
    for parity in range(2):
        c = cos_t[parity::2, : SIZE // 2]
        s = sin_t[parity::2, : SIZE // 2]
        table = np.block([[c, -s], [s, c]])
        found += [table, np.ascontiguousarray(table.T)]
    return np.stack(found)


def parity_order():
    order = np.concatenate([np.arange(0, SIZE, 2), np.arange(1, SIZE, 2)])
    right = np.arange(SIZE)[:, None] == order[None, :]
    return np.stack([right, right.T]).astype(BF16)


def dot(a, b):
    return jnp.dot(a, b, preferred_element_type=F32)


def grid_place():
    return lax.axis_index("row"), lax.axis_index("col")


def greet(peers):
    barrier = pltpu.get_barrier_semaphore()
    for peer in peers:
        pl.semaphore_signal(barrier, inc=1, device_id=peer, device_id_type=MESH)
    pl.semaphore_wait(barrier, len(peers))


def halo_kernel(rows, cols, obj_r, obj_i, amp, order, ext, amp_out, own_sem, send_sem, recv_sem):
    row, col = grid_place()
    up = (lax.rem(row + rows - 1, rows), col)
    down = (lax.rem(row + 1, rows), col)
    left = (row, lax.rem(col + cols - 1, cols))
    right = (row, lax.rem(col + 1, cols))
    greet((up, down, left, right))
    objs = (obj_r, obj_i)

    def band(part, j, number):
        return pltpu.make_async_remote_copy(
            src_ref=objs[part].at[pl.ds(0, SIZE), pl.ds(j * LANES, LANES)],
            dst_ref=ext.at[part, j, pl.ds(TILE, SIZE), :],
            send_sem=send_sem.at[number],
            recv_sem=recv_sem.at[number],
            device_id=up,
            device_id_type=MESH,
        )

    def side(part, j, number):
        return pltpu.make_async_remote_copy(
            src_ref=objs[part].at[:, pl.ds(j * LANES, LANES)],
            dst_ref=ext.at[part, 4 + j, pl.ds(0, TILE), :],
            send_sem=send_sem.at[number],
            recv_sem=recv_sem.at[number],
            device_id=left,
            device_id_type=MESH,
        )

    def corner(part, j, number):
        return pltpu.make_async_remote_copy(
            src_ref=ext.at[part, j, pl.ds(TILE, SIZE), :],
            dst_ref=ext.at[part, 4 + j, pl.ds(TILE, SIZE), :],
            send_sem=send_sem.at[number],
            recv_sem=recv_sem.at[number],
            device_id=left,
            device_id_type=MESH,
        )

    bands = [band(part, j, 2 * j + part) for j in range(4) for part in range(2)]
    sides = [side(part, j, 8 + 2 * j + part) for j in range(2) for part in range(2)]
    corners = [corner(part, j, 12 + 2 * j + part) for j in range(2) for part in range(2)]
    own = [
        pltpu.make_async_copy(
            objs[part].at[:, pl.ds(j * LANES, LANES)],
            ext.at[part, j, pl.ds(0, TILE), :],
            own_sem.at[2 * j + part],
        )
        for j in range(4)
        for part in range(2)
    ]
    for copy in bands + sides + own:
        copy.start()

    def sort(slot, carry):
        a = amp[slot]
        by_row = jnp.zeros((SIZE, SIZE), F32)
        for step in range(3):
            piece = a.astype(BF16)
            by_row += dot(order[1], piece)
            a = a - piece.astype(F32)
        total = jnp.zeros((SIZE, SIZE), F32)
        for step in range(3):
            piece = by_row.astype(BF16)
            total += dot(piece, order[0])
            by_row = by_row - piece.astype(F32)
        amp_out[slot] = total
        return carry

    lax.fori_loop(0, SLOTS, sort, 0)
    for number in range(4):
        bands[number].wait_recv()
        corners[number].start()
    for copy in own:
        copy.wait()
    for copy in bands:
        copy.wait_send()
    for copy in bands[4:]:
        copy.wait_recv()
    for copy in sides + corners:
        copy.wait()


def frames_kernel(
    pos, cnt, ext, amp, pr, pi, tab, acc, pg, pat_r, pat_i, xp, xq, far_e, far_o, inten, og_r, og_i
):
    half = SIZE // 2
    blank = jnp.zeros((SPAN, LANES), F32)
    for part in range(2):
        for j in range(6):
            acc[part, j] = blank
        for m in range(MODES):
            pg[part, m] = jnp.zeros((SIZE, SIZE), F32)

    def frame(s, carry):
        y = pos[2 * s]
        x = pos[2 * s + 1]
        jb = x // LANES
        sh = x % LANES
        back = (LANES - sh) % LANES
        lane = lax.broadcasted_iota(jnp.int32, (CHUNK, LANES), 1)
        keep = lane < LANES - sh
        for part, dst in ((0, pat_r), (1, pat_i)):
            for c in range(0, SIZE, CHUNK):
                a, b, d = (
                    pltpu.roll(ext[part, jb + t, pl.ds(y + c, CHUNK), :], back, 1) for t in range(3)
                )
                dst[c : c + CHUNK, :half] = jnp.where(keep, a, b)
                dst[c : c + CHUNK, half:] = jnp.where(keep, b, d)
        for m in range(MODES):
            for c in range(0, half, CHUNK):
                w = []
                for o in (c, c + half):
                    a, b = pr[m, o : o + CHUNK], pi[m, o : o + CHUNK]
                    u, v = pat_r[o : o + CHUNK], pat_i[o : o + CHUNK]
                    w.append((a * u - b * v, a * v + b * u))
                (tr, ti), (br, bi) = w
                xp[m, c : c + CHUNK] = (tr + br).astype(BF16)
                xp[m, c + half : c + half + CHUNK] = (ti + bi).astype(BF16)
                xq[m, c : c + CHUNK] = (tr - br).astype(BF16)
                xq[m, c + half : c + half + CHUNK] = (ti - bi).astype(BF16)
        for m in range(MODES):
            xe, xo = [], []
            for h in (dot(tab[0], xp[m]), dot(tab[2], xq[m])):
                hr, hi = h[:half], h[half:]
                xe.append(
                    jnp.concatenate(
                        [hr[:, :half] + hr[:, half:], hi[:, :half] + hi[:, half:]], axis=1
                    ).astype(BF16)
                )
                xo.append(
                    jnp.concatenate(
                        [hr[:, :half] - hr[:, half:], hi[:, :half] - hi[:, half:]], axis=1
                    ).astype(BF16)
                )
            fe = dot(jnp.concatenate(xe, axis=0), tab[1])
            fo = dot(jnp.concatenate(xo, axis=0), tab[3])
            far_e[m] = fe
            far_o[m] = fo
            te = fe[:, :half] * fe[:, :half] + fe[:, half:] * fe[:, half:]
            to = fo[:, :half] * fo[:, :half] + fo[:, half:] * fo[:, half:]
            if m == 0:
                inten[:, :half] = te
                inten[:, half:] = to
            else:
                inten[:, :half] += te
                inten[:, half:] += to
        for c in range(0, SIZE, CHUNK):
            rows = slice(c, c + CHUNK)
            inten[rows] = 1.0 - amp[s, rows] * lax.rsqrt(jnp.maximum(inten[rows], 0.25))
        for m in range(MODES):
            for p, dst in ((0, xp), (1, xq)):
                for c in range(0, half, CHUNK):
                    rows = slice(p * half + c, p * half + c + CHUNK)
                    f0, f1 = inten[rows, :half], inten[rows, half:]
                    e, o = far_e[m, rows], far_o[m, rows]
                    dst[m, c : c + CHUNK] = jnp.concatenate(
                        [e[:, :half] * f0, o[:, :half] * f1], axis=1
                    ).astype(BF16)
                    dst[m, c + half : c + half + CHUNK] = jnp.concatenate(
                        [e[:, half:] * f0, o[:, half:] * f1], axis=1
                    ).astype(BF16)
        for m in range(MODES):
            a = dot(tab[1], xp[m])
            b = dot(tab[3], xq[m])
            ur = jnp.concatenate([a[:half] + b[:half], a[:half] - b[:half]], axis=0).astype(BF16)
            ui = jnp.concatenate([a[half:] + b[half:], a[half:] - b[half:]], axis=0).astype(BF16)
            ga = dot(jnp.concatenate([ur[:, :half], ui[:, :half]], axis=1), tab[0])
            gb = dot(jnp.concatenate([ur[:, half:], ui[:, half:]], axis=1), tab[2])
            for c in range(0, SIZE, CHUNK):
                rows = slice(c, c + CHUNK)
                sm, df = ga[rows] + gb[rows], ga[rows] - gb[rows]
                gr = jnp.concatenate([sm[:, :half], df[:, :half]], axis=1)
                gi = jnp.concatenate([sm[:, half:], df[:, half:]], axis=1)
                a, b = pr[m, rows], pi[m, rows]
                u, v = pat_r[rows], pat_i[rows]
                obr = a * gr + b * gi
                obi = a * gi - b * gr
                if m == 0:
                    og_r[rows] = obr
                    og_i[rows] = obi
                else:
                    og_r[rows] += obr
                    og_i[rows] += obi
                pg[0, m, rows] += u * gr + v * gi
                pg[1, m, rows] += u * gi - v * gr
        low = lane < sh
        for part, src in ((0, og_r), (1, og_i)):
            for c in range(0, SIZE, CHUNK):
                a = pltpu.roll(src[c : c + CHUNK, :half], sh, 1)
                b = pltpu.roll(src[c : c + CHUNK, half:], sh, 1)
                acc[part, jb, pl.ds(y + c, CHUNK), :] += jnp.where(low, 0.0, a)
                acc[part, jb + 1, pl.ds(y + c, CHUNK), :] += jnp.where(low, a, b)
                acc[part, jb + 2, pl.ds(y + c, CHUNK), :] += jnp.where(low, b, 0.0)
        return carry

    lax.fori_loop(0, cnt[0], frame, 0)


def combine_kernel(
    rows,
    cols,
    step,
    acc,
    pg,
    obj_r,
    obj_i,
    pr,
    pi,
    new_r,
    new_i,
    new_pr,
    new_pi,
    tile,
    band,
    corner,
    side,
    below,
    data,
    result,
    rbuf0,
    rbuf1,
    rbuf2,
    rbuf3,
    local_sem,
    halo_send,
    halo_recv,
    sum_send,
    sum_recv,
):
    row, col = grid_place()
    n = 4
    core, x = lax.rem(col, 2), col // 2
    z, y = lax.rem(row, n), row // n
    up = (lax.rem(row + rows - 1, rows), col)
    down = (lax.rem(row + 1, rows), col)
    left = (row, lax.rem(col + cols - 1, cols))
    right = (row, lax.rem(col + 1, cols))
    other = (row, x * 2 + 1 - core)

    def peer(axis, k):
        if axis == "x":
            return (row, lax.rem(x + k, n) * 2 + core)
        if axis == "y":
            return (lax.rem(y + k, n) * n + z, col)
        return (y * n + lax.rem(z + k, n), col)

    where = {"x": x, "y": y, "z": z}
    peers = [peer(axis, k) for axis in "xyz" for k in (1, 2, 3)]

    loads = [
        pltpu.make_async_copy(pg, data, local_sem.at[0]),
        pltpu.make_async_copy(
            acc.at[:, pl.ds(0, 2), pl.ds(TILE, SIZE), :], band, local_sem.at[1]
        ),
        pltpu.make_async_copy(
            acc.at[:, pl.ds(0, 4), pl.ds(0, TILE), :], tile, local_sem.at[2]
        ),
    ]
    for copy in loads:
        copy.start()
    greet([up, down, left, right, other] + peers)

    def halo(src, dst, number, device):
        return pltpu.make_async_remote_copy(
            src_ref=src,
            dst_ref=dst,
            send_sem=halo_send.at[number],
            recv_sem=halo_recv.at[number],
            device_id=device,
            device_id_type=MESH,
        )

    corner_copy = halo(acc.at[:, pl.ds(4, 2), pl.ds(TILE, SIZE), :], corner, 0, right)
    far_copy = halo(
        acc.at[:, pl.ds(2, 2), pl.ds(TILE, SIZE), :], below.at[:, pl.ds(2, 2)], 1, down
    )
    near_copy = halo(band, below.at[:, pl.ds(0, 2)], 2, down)
    side_copy = halo(acc.at[:, pl.ds(4, 2), pl.ds(0, TILE), :], side, 3, right)
    corner_copy.start()
    far_copy.start()

    numbers = iter(range(64))

    def send(src, dst, device):
        number = next(numbers)
        copy = pltpu.make_async_remote_copy(
            src_ref=src,
            dst_ref=dst,
            send_sem=sum_send.at[number],
            recv_sem=sum_recv.at[number],
            device_id=device,
            device_id_type=MESH,
        )
        copy.start()
        return copy

    pending = []
    whole = 2 * MODES * SIZE
    kept = whole // 2
    mine = pl.multiple_of(core * kept, kept)
    theirs = pl.multiple_of((1 - core) * kept, kept)
    loads[0].wait()
    copy = send(data.at[pl.ds(theirs, kept), :], rbuf0, other)
    side_copy.start()
    copy.wait_recv()
    pending.append(copy)

    def add_up(base, length, buffers):
        size = min(length, 128)

        def body(i, carry):
            at = pl.multiple_of(base + i * size, 8)
            total = data[pl.ds(at, size), :]
            for ref, start in buffers:
                total += ref[pl.ds(pl.multiple_of(start + i * size, 8), size), :]
            data[pl.ds(at, size), :] = total
            return carry

        lax.fori_loop(0, length // size, body, 0)

    add_up(mine, kept, [(rbuf0, 0)])

    routes = ("yxz", "xyz")
    length = kept // len(routes)
    bases = [mine + part * length for part in range(len(routes))]
    trail = []
    for stage, buffer in enumerate((rbuf1, rbuf2, rbuf3)):
        quarter = length // n
        batch = []
        for part, route in enumerate(routes):
            axis = route[stage]
            p = where[axis]
            for k in (1, 2, 3):
                q = lax.rem(p + k, n)
                src = data.at[pl.ds(pl.multiple_of(bases[part] + q * quarter, 8), quarter), :]
                dst = buffer.at[pl.ds((part * 3 + k - 1) * quarter, quarter), :]
                batch.append(send(src, dst, peer(axis, k)))
        if stage == 0:
            loads[1].wait()
            corner_copy.wait_recv()
            for part in range(2):
                for j in range(2):
                    band[part, j] += corner[part, j]
            near_copy.start()
        trail.append(list(bases))
        for part, route in enumerate(routes):
            for k in range(3):
                batch[part * 3 + k].wait_recv()
            bases[part] = bases[part] + where[route[stage]] * quarter
            add_up(
                bases[part],
                quarter,
                [(buffer, (part * 3 + k) * quarter) for k in range(3)],
            )
        pending += batch
        length = quarter

    for part in range(len(routes)):
        at = pl.multiple_of(bases[part], 8)
        result[pl.ds(at, length), :] = data[pl.ds(at, length), :]
    for stage in (2, 1, 0):
        batch = []
        for part, route in enumerate(routes):
            axis = route[stage]
            for k in (1, 2, 3):
                here = result.at[pl.ds(pl.multiple_of(bases[part], 8), length), :]
                batch.append(send(here, here, peer(axis, k)))
        for copy in batch:
            copy.wait_recv()
        pending += batch
        bases = trail[stage]
        length *= n
    here = result.at[pl.ds(mine, kept), :]
    copy = send(here, here, other)
    pending.append(copy)

    far_copy.wait_recv()
    near_copy.wait_recv()
    side_copy.wait_recv()
    loads[2].wait()
    for part, obj, new in ((0, obj_r, new_r), (1, obj_i, new_i)):
        for j in range(4):
            lanes = slice(j * LANES, (j + 1) * LANES)
            for top in (0, SIZE):
                total = tile[part, j, top : top + SIZE]
                if top == 0:
                    total += below[part, j]
                if j < 2:
                    total += side[part, j, top : top + SIZE]
                new[top : top + SIZE, lanes] = obj[top : top + SIZE, lanes] - OBJECT_STEP * total

    copy.wait_recv()
    for part, old, new in ((0, pr, new_pr), (1, pi, new_pi)):
        for m in range(MODES):
            at = (part * MODES + m) * SIZE
            new[m] = old[m] - step * result[at : at + SIZE]
    for copy in pending:
        copy.wait_send()
    for copy in (corner_copy, far_copy, near_copy, side_copy):
        copy.wait_send()


def shards(object_real, object_imag, probe_real, probe_imag, amplitudes, positions, counts):
    rows, cols = lax.axis_size("row"), lax.axis_size("col")
    vmem = pl.BlockSpec(memory_space=pltpu.VMEM)
    smem = pl.BlockSpec(memory_space=pltpu.SMEM)
    anywhere = pl.BlockSpec(memory_space=pl.ANY)
    dma = pltpu.SemaphoreType.DMA
    extended = jax.ShapeDtypeStruct((2, 6, SPAN, LANES), F32)
    frame_shape = (SIZE, SIZE)

    ext, amp = pl.pallas_call(
        lambda *refs: halo_kernel(rows, cols, *refs),
        out_shape=(extended, jax.ShapeDtypeStruct((SLOTS, SIZE, SIZE), F32)),
        in_specs=[anywhere, anywhere, vmem, vmem],
        out_specs=(anywhere, vmem),
        scratch_shapes=[dma((8,)), dma((16,)), dma((16,))],
        compiler_params=pltpu.CompilerParams(
            collective_id=0, has_side_effects=True, vmem_limit_bytes=VMEM_LIMIT
        ),
        name="halo",
    )(object_real, object_imag, amplitudes[0, 0], jnp.asarray(parity_order()))

    acc, pg = pl.pallas_call(
        frames_kernel,
        out_shape=(extended, jax.ShapeDtypeStruct((2, MODES, SIZE, SIZE), F32)),
        in_specs=[smem, smem] + [vmem] * 5,
        out_specs=(vmem, vmem),
        scratch_shapes=[
            pltpu.VMEM(frame_shape, F32),
            pltpu.VMEM(frame_shape, F32),
            pltpu.VMEM((MODES, SIZE, SIZE), BF16),
            pltpu.VMEM((MODES, SIZE, SIZE), BF16),
            pltpu.VMEM((MODES, SIZE, SIZE), F32),
            pltpu.VMEM((MODES, SIZE, SIZE), F32),
            pltpu.VMEM(frame_shape, F32),
            pltpu.VMEM(frame_shape, F32),
            pltpu.VMEM(frame_shape, F32),
        ],
        compiler_params=pltpu.CompilerParams(vmem_limit_bytes=VMEM_LIMIT),
        name="frames",
    )(
        positions[0, 0].reshape(-1),
        counts.reshape(-1),
        ext,
        amp,
        probe_real,
        probe_imag,
        jnp.asarray(tables()),
    )

    step = PROBE_STEP / math.sqrt(SLOTS * rows * cols)
    tile_shape = jax.ShapeDtypeStruct((TILE, TILE), F32)
    probe_shape = jax.ShapeDtypeStruct((MODES, SIZE, SIZE), F32)
    whole = 2 * MODES * SIZE
    return pl.pallas_call(
        lambda *refs: combine_kernel(rows, cols, step, *refs),
        out_shape=(tile_shape, tile_shape, probe_shape, probe_shape),
        in_specs=[anywhere, anywhere] + [vmem] * 4,
        out_specs=(vmem,) * 4,
        scratch_shapes=[
            pltpu.VMEM((2, 4, TILE, LANES), F32),
            pltpu.VMEM((2, 2, SIZE, LANES), F32),
            pltpu.VMEM((2, 2, SIZE, LANES), F32),
            pltpu.VMEM((2, 2, TILE, LANES), F32),
            pltpu.VMEM((2, 4, SIZE, LANES), F32),
            pltpu.VMEM((whole, SIZE), F32),
            pltpu.VMEM((whole, SIZE), F32),
            pltpu.VMEM((whole // 2, SIZE), F32),
            pltpu.VMEM((whole // 2 * 3 // 4, SIZE), F32),
            pltpu.VMEM((whole // 8 * 3 // 4, SIZE), F32),
            pltpu.VMEM((whole // 32 * 3 // 4, SIZE), F32),
            dma((3,)),
            dma((4,)),
            dma((4,)),
            dma((38,)),
            dma((38,)),
        ],
        compiler_params=pltpu.CompilerParams(
            collective_id=1, has_side_effects=True, vmem_limit_bytes=VMEM_LIMIT
        ),
        name="combine",
    )(
        acc,
        pg.reshape(whole, SIZE),
        object_real,
        object_imag,
        probe_real,
        probe_imag,
    )


def solution(mesh):
    in_specs = (
        P("row", "col"),
        P("row", "col"),
        P(),
        P(),
        P("row", "col", None, None, None),
        P("row", "col", None, None),
        P("row", "col"),
    )
    out_specs = (P("row", "col"), P("row", "col"), P(), P())
    return jax.shard_map(shards, mesh=mesh, in_specs=in_specs, out_specs=out_specs, check_vma=False)
```

profile of v0, /device:TPU:1, one launch (start us, length us, event | category | flops | bytes accessed | tf_op | source)
XLA Modules:
  0.0 172.5 jit_solution(9360745859043544480)
XLA Ops:
  1.3 0.8 copy.14
  2.0 0.6 reshape_squeeze.3.pos
  2.6 75.1 %halo.1 = (f32[2,6,768,128]{3,2,1,0:T(8,128)}, f32[8,256,256]{2,1,0:T(8,128)}) custom-call(f32[512,512]{1,0:T(8,128)} %refs_2_.1, f32[512,512]{1,0:T(8,128)} %refs_3_.2, f32[8,256,256]{2,1,0:T(8,128)} %bitcast.6, bf16[2,256,256]{2,1,0:T(8,128)(2,1)} %constant.4.clone.refs_3_), custom_call_target="tpu_custom_call" | custom-call | tf_op jit(solution)/shard_map/halo/pallas_call | solution.py:474
  77.7 10.0 %frames.1 = (f32[2,6,768,128]{3,2,1,0:T(8,128)}, f32[2,4,256,256]{3,2,1,0:T(8,128)}) custom-call(s32[16]{0:T(128)} %reshape_squeeze.3.pos, s32[1]{0:T(128)} %bitcast.5.cnt, f32[2,6,768,128]{3,2,1,0:T(8,128)} %get-tuple-element.8.ext, f32[8,256,256]{2,1,0:T(8,128)} %get-tuple-element.9.amp, f32[4,256,256]{2,1,0:T(8,128)} %refs_4_.1, f32[4,256,256]{2,1,0:T(8,128)} %refs_5_.1, ...), custom_call_target="tpu_custom_call" | custom-call | tf_op jit(solution)/shard_map/frames/pallas_call | solution.py:486
  87.7 79.5 %combine.1 = (f32[512,512]{1,0:T(8,128)}, f32[512,512]{1,0:T(8,128)}, f32[4,256,256]{2,1,0:T(8,128)}, f32[4,256,256]{2,1,0:T(8,128)}) custom-call(f32[2,6,768,128]{3,2,1,0:T(8,128)} %get-tuple-element.10.refs_0_, f32[2048,256]{1,0:T(8,128)} %bitcast.7, f32[512,512]{1,0:T(8,128)} %refs_2_.1, f32[512,512]{1,0:T(8,128)} %refs_3_.2, f32[4,256,256]{2,1,0:T(8,128)} %refs_4_.1, ...), custom_call_target="tpu_custom_call" | custom-call | tf_op jit(solution)/shard_map/combine/pallas_call | solution.py:518
  167.2 0.0 copy-start.2
  167.2 0.0 copy-start.1
  167.2 2.4 %copy.20 = f32[512,512]{1,0:T(8,128)} copy(f32[512,512]{1,0:T(8,128)} %get-tuple-element.16) | data formatting | bytes 2097152
  169.6 0.0 copy-done.2
  169.6 0.0 copy-start
  169.6 1.0 copy.21
  170.6 0.0 copy-done.1
  170.6 1.0 copy.22
  171.6 0.0 copy-done
  171.6 1.0 copy.23
Async XLA Ops:
  167.2 2.4 %copy-start.2 = (f32[512,512]{1,0:T(8,128)S(1)}, f32[512,512]{1,0:T(8,128)}, u32[]{:S(2)}) copy-start(f32[512,512]{1,0:T(8,128)} %get-tuple-element.17) | copy-start | bytes 3145732
  167.2 3.4 %copy-start.1 = (f32[4,256,256]{2,1,0:T(8,128)S(1)}, f32[4,256,256]{2,1,0:T(8,128)}, u32[]{:S(2)}) copy-start(f32[4,256,256]{2,1,0:T(8,128)} %get-tuple-element.18) | copy-start | bytes 3145732
  169.6 1.9 %copy-start = (f32[4,256,256]{2,1,0:T(8,128)S(1)}, f32[4,256,256]{2,1,0:T(8,128)}, u32[]{:S(2)}) copy-start(f32[4,256,256]{2,1,0:T(8,128)} %get-tuple-element.19) | copy-start | bytes 3145732
where the time goes:
time: 173 us
  Pallas kernels  165 us (95%)
  local copies, waits for them, and re-layouts  6.68 us (4%)
    pallas_call x1, Pallas kernels, shards(): pl.pallas_call(lambda *refs: combine_kernel(rows, cols, step, *refs), out...  79.5 us
    pallas_call x1, Pallas kernels, shards(): pl.pallas_call(lambda *refs: halo_kernel(rows, cols, *refs), out_shape=(e...  75.1 us
    pallas_call x1, Pallas kernels, shards(): pl.pallas_call(frames_kernel, out_shape=(extended, jax.ShapeDtypeStruct((...  10 us
    unnamed x11, local copies, waits for them, and re-layouts  6.09 us

commit v1 on v0

v1 whole, which is shorter than its diff:
```python
import math

import jax
import jax.numpy as jnp
import numpy as np
from jax import lax
from jax.experimental import pallas as pl
from jax.experimental.pallas import tpu as pltpu
from jax.sharding import PartitionSpec as P

OBJECT_STEP = 0.25
PROBE_STEP = 0.5
MESH = pl.DeviceIdType.MESH
F32 = jnp.float32
BF16 = jnp.bfloat16
LANES = 128
SIZE = 256
MODES = 4
TILE = 512
SPAN = TILE + SIZE
SLOTS = 8
CHUNK = 32
VMEM_LIMIT = 56 * 2**20
SCHEDULE = (
    ("corner", ("far", 0)),
    (),
    (("side", 0),),
    (),
    (("far", 1), ("near", 0)),
    (("near", 1), ("side", 1)),
)


def tables():
    index = np.arange(SIZE)
    angle = (index[:, None] * index[None, :] % SIZE) * (2.0 * math.pi / SIZE)
    scale = 1.0 / math.sqrt(SIZE)
    cos_t = (np.cos(angle) * scale).astype(BF16)
    sin_t = (-np.sin(angle) * scale).astype(BF16)
    found = []
    for parity in range(2):
        c = cos_t[parity::2, : SIZE // 2]
        s = sin_t[parity::2, : SIZE // 2]
        table = np.block([[c, -s], [s, c]])
        found += [table, np.ascontiguousarray(table.T)]
    return np.stack(found)


def parity_order():
    order = np.concatenate([np.arange(0, SIZE, 2), np.arange(1, SIZE, 2)])
    right = np.arange(SIZE)[:, None] == order[None, :]
    return np.stack([right, right.T]).astype(BF16)


def dot(a, b):
    return jnp.dot(a, b, preferred_element_type=F32)


def grid_place():
    return lax.axis_index("row"), lax.axis_index("col")


def greet(peers):
    barrier = pltpu.get_barrier_semaphore()
    for peer in peers:
        pl.semaphore_signal(barrier, inc=1, device_id=peer, device_id_type=MESH)
    pl.semaphore_wait(barrier, len(peers))


def halo_kernel(rows, cols, obj_r, obj_i, amp, order, lower, wide, amp_out, send_sem, recv_sem):
    row, col = grid_place()
    up = (lax.rem(row + rows - 1, rows), col)
    down = (lax.rem(row + 1, rows), col)
    left = (row, lax.rem(col + cols - 1, cols))
    right = (row, lax.rem(col + 1, cols))
    greet((up, down, left, right))
    objs = (obj_r, obj_i)

    def band(part, j, number):
        return pltpu.make_async_remote_copy(
            src_ref=objs[part].at[pl.ds(0, SIZE), pl.ds(j * LANES, LANES)],
            dst_ref=lower.at[part, j],
            send_sem=send_sem.at[number],
            recv_sem=recv_sem.at[number],
            device_id=up,
            device_id_type=MESH,
        )

    def side(part, j, number):
        return pltpu.make_async_remote_copy(
            src_ref=objs[part].at[:, pl.ds(j * LANES, LANES)],
            dst_ref=wide.at[part, j, pl.ds(0, TILE), :],
            send_sem=send_sem.at[number],
            recv_sem=recv_sem.at[number],
            device_id=left,
            device_id_type=MESH,
        )

    def corner(part, j, number):
        return pltpu.make_async_remote_copy(
            src_ref=lower.at[part, j],
            dst_ref=wide.at[part, j, pl.ds(TILE, SIZE), :],
            send_sem=send_sem.at[number],
            recv_sem=recv_sem.at[number],
            device_id=left,
            device_id_type=MESH,
        )

    bands = [band(part, j, 2 * j + part) for j in range(4) for part in range(2)]
    sides = [side(part, j, 8 + 2 * j + part) for j in range(2) for part in range(2)]
    corners = [corner(part, j, 12 + 2 * j + part) for j in range(2) for part in range(2)]
    for copy in bands + sides:
        copy.start()

    def sort(slot, carry):
        a = amp[slot]
        by_row = jnp.zeros((SIZE, SIZE), F32)
        for step in range(3):
            piece = a.astype(BF16)
            by_row += dot(order[1], piece)
            a = a - piece.astype(F32)
        total = jnp.zeros((SIZE, SIZE), F32)
        for step in range(3):
            piece = by_row.astype(BF16)
            total += dot(piece, order[0])
            by_row = by_row - piece.astype(F32)
        amp_out[slot] = total
        return carry

    lax.fori_loop(0, SLOTS, sort, 0)
    for number in range(4):
        bands[number].wait_recv()
        corners[number].start()
    for copy in bands:
        copy.wait_send()
    for copy in bands[4:]:
        copy.wait_recv()
    for copy in sides + corners:
        copy.wait()


def frames_kernel(
    pos,
    cnt,
    obj_r,
    obj_i,
    lower,
    wide,
    amp,
    pr,
    pi,
    tab,
    acc,
    pg,
    ext,
    pat_r,
    pat_i,
    xp,
    xq,
    xe,
    xo,
    far_e,
    far_o,
    inten,
    og_r,
    og_i,
    sem,
):
    half = SIZE // 2
    loads = [
        pltpu.make_async_copy(lower, ext.at[:, pl.ds(0, 4), pl.ds(TILE, SIZE), :], sem.at[0]),
        pltpu.make_async_copy(wide, ext.at[:, pl.ds(4, 2)], sem.at[1]),
    ]
    for part, obj in ((0, obj_r), (1, obj_i)):
        for j in range(4):
            loads.append(
                pltpu.make_async_copy(
                    obj.at[:, pl.ds(j * LANES, LANES)],
                    ext.at[part, j, pl.ds(0, TILE), :],
                    sem.at[2 + 4 * part + j],
                )
            )
    for copy in loads:
        copy.start()
    blank = jnp.zeros((SPAN, LANES), F32)
    for part in range(2):
        for j in range(6):
            acc[part, j] = blank
        for m in range(MODES):
            pg[part, m] = jnp.zeros((SIZE, SIZE), F32)
    for copy in loads:
        copy.wait()

    def frame(s, carry):
        y = pos[2 * s]
        x = pos[2 * s + 1]
        jb = x // LANES
        sh = x % LANES
        back = (LANES - sh) % LANES
        lane = lax.broadcasted_iota(jnp.int32, (CHUNK, LANES), 1)
        keep = lane < LANES - sh
        for part, dst in ((0, pat_r), (1, pat_i)):
            for c in range(0, SIZE, CHUNK):
                a, b, d = (
                    pltpu.roll(ext[part, jb + t, pl.ds(y + c, CHUNK), :], back, 1) for t in range(3)
                )
                dst[c : c + CHUNK, :half] = jnp.where(keep, a, b)
                dst[c : c + CHUNK, half:] = jnp.where(keep, b, d)
        for m in range(MODES):
            for c in range(0, half, CHUNK):
                w = []
                for o in (c, c + half):
                    a, b = pr[m, o : o + CHUNK], pi[m, o : o + CHUNK]
                    u, v = pat_r[o : o + CHUNK], pat_i[o : o + CHUNK]
                    w.append((a * u - b * v, a * v + b * u))
                (tr, ti), (br, bi) = w
                xp[m, c : c + CHUNK] = (tr + br).astype(BF16)
                xp[m, c + half : c + half + CHUNK] = (ti + bi).astype(BF16)
                xq[m, c : c + CHUNK] = (tr - br).astype(BF16)
                xq[m, c + half : c + half + CHUNK] = (ti - bi).astype(BF16)
        for m in range(MODES):
            for p, src in ((0, xp), (1, xq)):
                h = dot(tab[2 * p], src[m])
                rows = slice(m * SIZE + p * half, m * SIZE + (p + 1) * half)
                for part in range(2):
                    first, second = h[part * half : (part + 1) * half, :half], h[part * half : (part + 1) * half, half:]
                    lanes = slice(part * half, (part + 1) * half)
                    xe[rows, lanes] = (first + second).astype(BF16)
                    xo[rows, lanes] = (first - second).astype(BF16)
        far_e[...] = dot(xe[...], tab[1]).reshape(MODES, SIZE, SIZE)
        far_o[...] = dot(xo[...], tab[3]).reshape(MODES, SIZE, SIZE)
        for c in range(0, SIZE, CHUNK):
            rows = slice(c, c + CHUNK)
            for far, lanes in ((far_e, slice(0, half)), (far_o, slice(half, SIZE))):
                total = None
                for m in range(MODES):
                    f = far[m, rows]
                    f = f * f
                    f = f[:, :half] + f[:, half:]
                    total = f if total is None else total + f
                inten[rows, lanes] = 1.0 - amp[s, rows, lanes] * lax.rsqrt(jnp.maximum(total, 0.25))
        for m in range(MODES):
            for p, dst in ((0, xp), (1, xq)):
                for c in range(0, half, CHUNK):
                    rows = slice(p * half + c, p * half + c + CHUNK)
                    f0, f1 = inten[rows, :half], inten[rows, half:]
                    e, o = far_e[m, rows], far_o[m, rows]
                    dst[m, c : c + CHUNK] = jnp.concatenate(
                        [e[:, :half] * f0, o[:, :half] * f1], axis=1
                    ).astype(BF16)
                    dst[m, c + half : c + half + CHUNK] = jnp.concatenate(
                        [e[:, half:] * f0, o[:, half:] * f1], axis=1
                    ).astype(BF16)
        for m in range(MODES):
            a = dot(tab[1], xp[m])
            b = dot(tab[3], xq[m])
            for p, v in ((0, a + b), (1, a - b)):
                v = v.astype(BF16)
                rows = slice(m * SIZE + p * half, m * SIZE + (p + 1) * half)
                xe[rows, :half] = v[:half, :half]
                xe[rows, half:] = v[half:, :half]
                xo[rows, :half] = v[:half, half:]
                xo[rows, half:] = v[half:, half:]
        far_e[...] = dot(xe[...], tab[0]).reshape(MODES, SIZE, SIZE)
        far_o[...] = dot(xo[...], tab[2]).reshape(MODES, SIZE, SIZE)
        for c in range(0, SIZE, CHUNK):
            rows = slice(c, c + CHUNK)
            u, v = pat_r[rows], pat_i[rows]
            sum_r = sum_i = None
            for m in range(MODES):
                ga, gb = far_e[m, rows], far_o[m, rows]
                sm, df = ga + gb, ga - gb
                gr = jnp.concatenate([sm[:, :half], df[:, :half]], axis=1)
                gi = jnp.concatenate([sm[:, half:], df[:, half:]], axis=1)
                a, b = pr[m, rows], pi[m, rows]
                obr = a * gr + b * gi
                obi = a * gi - b * gr
                sum_r = obr if sum_r is None else sum_r + obr
                sum_i = obi if sum_i is None else sum_i + obi
                pg[0, m, rows] += u * gr + v * gi
                pg[1, m, rows] += u * gi - v * gr
            og_r[rows] = sum_r
            og_i[rows] = sum_i
        low = lane < sh
        for part, src in ((0, og_r), (1, og_i)):
            for c in range(0, SIZE, CHUNK):
                a = pltpu.roll(src[c : c + CHUNK, :half], sh, 1)
                b = pltpu.roll(src[c : c + CHUNK, half:], sh, 1)
                acc[part, jb, pl.ds(y + c, CHUNK), :] += jnp.where(low, 0.0, a)
                acc[part, jb + 1, pl.ds(y + c, CHUNK), :] += jnp.where(low, a, b)
                acc[part, jb + 2, pl.ds(y + c, CHUNK), :] += jnp.where(low, b, 0.0)
        return carry

    lax.fori_loop(0, cnt[0], frame, 0)


def combine_kernel(
    rows,
    cols,
    acc,
    pg,
    below,
    side,
    result,
    band,
    corner,
    data,
    rbuf0,
    rbuf1,
    rbuf2,
    local_sem,
    halo_send,
    halo_recv,
    sum_send,
    sum_recv,
):
    row, col = grid_place()
    n = 4
    core, x = lax.rem(col, 2), col // 2
    z, y = lax.rem(row, n), row // n
    up = (lax.rem(row + rows - 1, rows), col)
    down = (lax.rem(row + 1, rows), col)
    left = (row, lax.rem(col + cols - 1, cols))
    right = (row, lax.rem(col + 1, cols))
    other = (row, x * 2 + 1 - core)

    def at_place(dx, dy, dz):
        return (
            lax.rem(y + dy, n) * n + lax.rem(z + dz, n),
            lax.rem(x + dx, n) * 2 + core,
        )

    steps = [(a, b) for a in range(n) for b in range(n) if a or b]
    lines = ([at_place(0, k, 0) for k in (1, 2, 3)], [at_place(k, 0, 0) for k in (1, 2, 3)])
    planes = ([at_place(a, 0, b) for a, b in steps], [at_place(0, a, b) for a, b in steps])
    line_at = (y, x)
    plane_at = (x, y)

    loads = [
        pltpu.make_async_copy(pg, data, local_sem.at[0]),
        pltpu.make_async_copy(
            acc.at[:, pl.ds(0, 2), pl.ds(TILE, SIZE), :], band, local_sem.at[1]
        ),
    ]
    for copy in loads:
        copy.start()
    greet(
        [up, down, left, right, other]
        + planes[0]
        + [p for p, (a, b) in zip(planes[1], steps) if a]
    )

    def halo(src, dst, number, device):
        return pltpu.make_async_remote_copy(
            src_ref=src,
            dst_ref=dst,
            send_sem=halo_send.at[number],
            recv_sem=halo_recv.at[number],
            device_id=device,
            device_id_type=MESH,
        )

    corner_copy = halo(acc.at[:, pl.ds(4, 2), pl.ds(TILE, SIZE), :], corner, 0, right)
    moves = {"corner": corner_copy}
    for part in range(2):
        moves["far", part] = halo(
            acc.at[part, pl.ds(2, 2), pl.ds(TILE, SIZE), :], below.at[part, pl.ds(2, 2)], 1 + part, down
        )
        moves["near", part] = halo(band.at[part], below.at[part, pl.ds(0, 2)], 3 + part, down)
        moves["side", part] = halo(
            acc.at[part, pl.ds(4, 2), pl.ds(0, TILE), :], side.at[part], 5 + part, right
        )

    def begin(stage):
        for name in SCHEDULE[stage]:
            moves[name].start()

    begin(0)

    numbers = iter(range(82))
    pending = []

    def send(src, dst, device):
        number = next(numbers)
        copy = pltpu.make_async_remote_copy(
            src_ref=src,
            dst_ref=dst,
            send_sem=sum_send.at[number],
            recv_sem=sum_recv.at[number],
            device_id=device,
            device_id_type=MESH,
        )
        copy.start()
        pending.append(copy)
        return copy

    def aligned(start, size):
        return pl.ds(pl.multiple_of(start, 8), size)

    whole = 2 * MODES * SIZE
    kept = whole // 2
    part_rows = kept // 2
    quarter = part_rows // n
    piece = quarter // (n * n)
    mine = core * kept
    theirs = (1 - core) * kept
    loads[0].wait()
    core_copies = [
        send(
            data.at[aligned(theirs + part * part_rows, part_rows), :],
            rbuf0.at[pl.ds(part * part_rows, part_rows), :],
            other,
        )
        for part in range(2)
    ]

    begin(1)
    line_copies = []
    for part in range(2):
        core_copies[part].wait_recv()
        base = mine + part * part_rows

        def add_core(i, carry, base=base, part=part):
            here = aligned(base + i * quarter, quarter)
            data[here, :] += rbuf0[pl.ds(pl.multiple_of(part * part_rows + i * quarter, 8), quarter), :]
            return carry

        lax.fori_loop(0, n, add_core, 0)
        for k in (1, 2, 3):
            q = lax.rem(line_at[part] + k, n)
            line_copies.append(
                send(
                    data.at[aligned(base + q * quarter, quarter), :],
                    rbuf1.at[pl.ds((part * 3 + k - 1) * quarter, quarter), :],
                    lines[part][k - 1],
                )
            )

    loads[1].wait()
    corner_copy.wait_recv()
    for part in range(2):
        for j in range(2):
            band[part, j] += corner[part, j]
    begin(2)

    bases = []
    plane_copies = []
    for part in range(2):
        for k in range(3):
            line_copies[part * 3 + k].wait_recv()
        base = mine + part * part_rows + line_at[part] * quarter
        bases.append(base)
        here = aligned(base, quarter)
        total = data[here, :]
        for k in range(3):
            total += rbuf1[(part * 3 + k) * quarter : (part * 3 + k + 1) * quarter, :]
        data[here, :] = total
        for k, (a, b) in enumerate(steps):
            q = lax.rem(plane_at[part] + a, n) * n + lax.rem(z + b, n)
            plane_copies.append(
                send(
                    data.at[aligned(base + q * piece, piece), :],
                    rbuf2.at[pl.ds((part * 15 + k) * piece, piece), :],
                    planes[part][k],
                )
            )
    begin(3)

    gather_copies = []
    for part in range(2):
        for k in range(15):
            plane_copies[part * 15 + k].wait_recv()
        here = aligned(bases[part] + (plane_at[part] * n + z) * piece, piece)
        total = data[here, :]
        for k in range(15):
            total += rbuf2[(part * 15 + k) * piece : (part * 15 + k + 1) * piece, :]
        result[here, :] = total
        for k in range(15):
            gather_copies.append(
                send(result.at[here, :], result.at[here, :], planes[part][k])
            )

    begin(4)
    line_copies = []
    for part in range(2):
        for k in range(15):
            gather_copies[part * 15 + k].wait_recv()
        here = result.at[aligned(bases[part], quarter), :]
        for k in (1, 2, 3):
            line_copies.append(send(here, here, lines[part][k - 1]))
    core_copies = []
    for part in range(2):
        here = result.at[aligned(bases[part], quarter), :]
        core_copies.append(send(here, here, other))
    begin(5)
    for k in (1, 3, 2):
        for part in range(2):
            line_copies[part * 3 + k - 1].wait_recv()
            q = lax.rem(line_at[part] + n - k, n)
            here = result.at[aligned(mine + part * part_rows + q * quarter, quarter), :]
            core_copies.append(send(here, here, other))
    for copy in core_copies:
        copy.wait_recv()
    for copy in pending:
        copy.wait_send()
    for name, copy in moves.items():
        if name != "corner":
            copy.wait_recv()
    for copy in moves.values():
        copy.wait_send()


def finish_kernel(step, acc, below, side, result, obj_r, obj_i, pr, pi, new_r, new_i, new_pr, new_pi):
    upper = pl.program_id(0) < 2
    for part, obj, new in ((0, obj_r, new_r), (1, obj_i, new_i)):
        for j in range(4):
            lanes = slice(j * LANES, (j + 1) * LANES)
            total = acc[part, j] + jnp.where(upper, below[part, j], 0.0)
            if j < 2:
                total += side[part, j]
            new[:, lanes] = obj[:, lanes] - OBJECT_STEP * total
    for part, old, new in ((0, pr, new_pr), (1, pi, new_pi)):
        new[0] = old[0] - step * result[part, 0]


def shards(object_real, object_imag, probe_real, probe_imag, amplitudes, positions, counts):
    rows, cols = lax.axis_size("row"), lax.axis_size("col")
    vmem = pl.BlockSpec(memory_space=pltpu.VMEM)
    smem = pl.BlockSpec(memory_space=pltpu.SMEM)
    anywhere = pl.BlockSpec(memory_space=pl.ANY)
    dma = pltpu.SemaphoreType.DMA
    extended = jax.ShapeDtypeStruct((2, 6, SPAN, LANES), F32)
    frame_shape = (SIZE, SIZE)

    lower, wide, amp = pl.pallas_call(
        lambda *refs: halo_kernel(rows, cols, *refs),
        out_shape=(
            jax.ShapeDtypeStruct((2, 4, SIZE, LANES), F32),
            jax.ShapeDtypeStruct((2, 2, SPAN, LANES), F32),
            jax.ShapeDtypeStruct((SLOTS, SIZE, SIZE), F32),
        ),
        in_specs=[anywhere, anywhere, vmem, vmem],
        out_specs=(anywhere, anywhere, vmem),
        scratch_shapes=[dma((16,)), dma((16,))],
        compiler_params=pltpu.CompilerParams(
            collective_id=0, has_side_effects=True, vmem_limit_bytes=16 * 2**20
        ),
        name="halo",
    )(object_real, object_imag, amplitudes[0, 0], jnp.asarray(parity_order()))

    acc, pg = pl.pallas_call(
        frames_kernel,
        out_shape=(extended, jax.ShapeDtypeStruct((2, MODES, SIZE, SIZE), F32)),
        in_specs=[smem, smem] + [anywhere] * 4 + [vmem] * 4,
        out_specs=(vmem, vmem),
        scratch_shapes=[
            pltpu.VMEM((2, 6, SPAN, LANES), F32),
            pltpu.VMEM(frame_shape, F32),
            pltpu.VMEM(frame_shape, F32),
            pltpu.VMEM((MODES, SIZE, SIZE), BF16),
            pltpu.VMEM((MODES, SIZE, SIZE), BF16),
            pltpu.VMEM((MODES * SIZE, SIZE), BF16),
            pltpu.VMEM((MODES * SIZE, SIZE), BF16),
            pltpu.VMEM((MODES, SIZE, SIZE), F32),
            pltpu.VMEM((MODES, SIZE, SIZE), F32),
            pltpu.VMEM(frame_shape, F32),
            pltpu.VMEM(frame_shape, F32),
            pltpu.VMEM(frame_shape, F32),
            dma((10,)),
        ],
        compiler_params=pltpu.CompilerParams(vmem_limit_bytes=32 * 2**20),
        name="frames",
    )(
        positions[0, 0].reshape(-1),
        counts.reshape(-1),
        object_real,
        object_imag,
        lower,
        wide,
        amp,
        probe_real,
        probe_imag,
        jnp.asarray(tables()),
    )

    step = PROBE_STEP / math.sqrt(SLOTS * rows * cols)
    tile_shape = jax.ShapeDtypeStruct((TILE, TILE), F32)
    probe_shape = jax.ShapeDtypeStruct((MODES, SIZE, SIZE), F32)
    whole = 2 * MODES * SIZE
    below, side, result = pl.pallas_call(
        lambda *refs: combine_kernel(rows, cols, *refs),
        out_shape=(
            jax.ShapeDtypeStruct((2, 4, SIZE, LANES), F32),
            jax.ShapeDtypeStruct((2, 2, TILE, LANES), F32),
            jax.ShapeDtypeStruct((whole, SIZE), F32),
        ),
        in_specs=[anywhere, anywhere],
        out_specs=(anywhere, anywhere, vmem),
        scratch_shapes=[
            pltpu.VMEM((2, 2, SIZE, LANES), F32),
            pltpu.VMEM((2, 2, SIZE, LANES), F32),
            pltpu.VMEM((whole, SIZE), F32),
            pltpu.VMEM((whole // 2, SIZE), F32),
            pltpu.VMEM((whole // 2 * 3 // 4, SIZE), F32),
            pltpu.VMEM((30 * whole // 256, SIZE), F32),
            dma((2,)),
            dma((7,)),
            dma((7,)),
            dma((82,)),
            dma((82,)),
        ],
        compiler_params=pltpu.CompilerParams(
            collective_id=1, has_side_effects=True, vmem_limit_bytes=16 * 2**20
        ),
        name="combine",
    )(acc, pg.reshape(whole, SIZE))

    part = TILE // 4
    tile_block = pl.BlockSpec((part, TILE), lambda i: (i, 0))
    probe_block = pl.BlockSpec((1, SIZE, SIZE), lambda i: (i, 0, 0))
    return pl.pallas_call(
        lambda *refs: finish_kernel(step, *refs),
        grid=(4,),
        out_shape=(tile_shape, tile_shape, probe_shape, probe_shape),
        in_specs=[
            pl.BlockSpec((2, 4, part, LANES), lambda i: (0, 0, i, 0)),
            pl.BlockSpec((2, 4, part, LANES), lambda i: (0, 0, jnp.minimum(i, 1), 0)),
            pl.BlockSpec((2, 2, part, LANES), lambda i: (0, 0, i, 0)),
            pl.BlockSpec((2, 1, SIZE, SIZE), lambda i: (0, i, 0, 0)),
            tile_block,
            tile_block,
            probe_block,
            probe_block,
        ],
        out_specs=(tile_block, tile_block, probe_block, probe_block),
        compiler_params=pltpu.CompilerParams(vmem_limit_bytes=16 * 2**20),
        name="finish",
    )(
        acc,
        below,
        side,
        result.reshape(2, MODES, SIZE, SIZE),
        object_real,
        object_imag,
        probe_real,
        probe_imag,
    )


def solution(mesh):
    in_specs = (
        P("row", "col"),
        P("row", "col"),
        P(),
        P(),
        P("row", "col", None, None, None),
        P("row", "col", None, None),
        P("row", "col"),
    )
    out_specs = (P("row", "col"), P("row", "col"), P(), P())
    return jax.shard_map(shards, mesh=mesh, in_specs=in_specs, out_specs=out_specs, check_vma=False)
```

time: 173 us -> 118 us (0.68)
  Pallas kernels: 165 us -> 110 us
    pallas_call x2 -> x3, Pallas kernels: 155 us -> 97.8 us  [the longest x1 65.4 us: shards(): pl.pallas_call(lambda *refs: combine_kernel(rows, cols, *refs), out_shape...]
    pallas_call x1, Pallas kernels: 10 us -> 12.1 us  [shards(): pl.pallas_call(frames_kernel, out_shape=(extended, jax.ShapeDtypeStruct((...]
    unnamed x11 -> x19, local copies, waits for them, and re-layouts: 6.09 us -> 6.8 us
where the time goes in v1:
time: 118 us
  Pallas kernels  110 us (93%)
  local copies, waits for them, and re-layouts  6.88 us (6%)
  between operations  1.35 us (1%)
    pallas_call x1, Pallas kernels, shards(): pl.pallas_call(lambda *refs: combine_kernel(rows, cols, *refs), out_shape...  65.4 us
    pallas_call x1, Pallas kernels, shards(): pl.pallas_call(lambda *refs: halo_kernel(rows, cols, *refs), out_shape=(j...  29.3 us
    pallas_call x1, Pallas kernels, shards(): pl.pallas_call(frames_kernel, out_shape=(extended, jax.ShapeDtypeStruct((...  12.1 us
    unnamed x19, local copies, waits for them, and re-layouts  6.8 us
    pallas_call x1, Pallas kernels, shards(): pl.pallas_call(lambda *refs: finish_kernel(step, *refs), grid=(4,), out_s...  3.03 us

profile of v1, /device:TPU:1, one launch (start us, length us, event | category | flops | bytes accessed | tf_op | source)
XLA Modules:
  0.0 118.1 jit_solution(8701508053734704090)
XLA Ops:
  1.3 0.8 copy.14
  2.0 0.1 reshape_squeeze.3.pos
  2.1 0.0 copy-start
  2.1 1.2 %copy-done = f32[512,512]{1,0:T(8,128)S(1)} copy-done((f32[512,512]{1,0:T(8,128)S(1)}, f32[512,512]{1,0:T(8,128)}, u32[]{:S(2)}) %copy-start) | copy-done | bytes 1048600
  3.3 0.0 copy-start.2
  3.3 1.2 %copy-done.2 = f32[512,512]{1,0:T(8,128)S(1)} copy-done((f32[512,512]{1,0:T(8,128)S(1)}, f32[512,512]{1,0:T(8,128)}, u32[]{:S(2)}) %copy-start.2) | copy-done | bytes 1048600
  4.6 0.0 copy-start.6
  4.6 1.6 %copy-done.6 = f32[1,1,8,256,256]{4,3,2,1,0:T(8,128)S(1)} copy-done((f32[1,1,8,256,256]{4,3,2,1,0:T(8,128)S(1)}, f32[1,1,8,256,256]{4,3,2,1,0:T(8,128)}, u32[]{:S(2)}) %copy-start.6) | copy-done | bytes 2097176
  6.2 0.0 copy-start.8
  6.2 0.9 copy-done.8
  7.1 0.0 copy-start.1
  7.1 0.0 copy-start.3
  7.1 0.0 copy-start.4
  7.1 0.0 copy-start.5
  7.1 29.3 %halo.1 = (f32[2,4,256,128]{3,2,1,0:T(8,128)S(1)}, f32[2,2,768,128]{3,2,1,0:T(8,128)S(1)}, f32[8,256,256]{2,1,0:T(8,128)S(1)}) custom-call(f32[512,512]{1,0:T(8,128)S(1)} %copy-done, f32[512,512]{1,0:T(8,128)S(1)} %copy-done.2, f32[8,256,256]{2,1,0:T(8,128)S(1)} %bitcast.8, bf16[2,256,256]{2,1,0:T(8,128)(2,1)S(1)} %copy-done.8), custom_call_target="tpu_custom_call" | custom-call | tf_op jit(solution)/shard_map/halo/pallas_call | solution.py:535
  36.4 0.0 copy-done.1
  36.4 0.0 copy-done.3
  36.4 0.0 copy-done.4
  36.4 0.0 copy-done.5
  36.4 0.0 copy-start.7
  36.5 1.0 copy-done.7
  37.5 12.1 %frames.1 = (f32[2,6,768,128]{3,2,1,0:T(8,128)S(1)}, f32[2,4,256,256]{3,2,1,0:T(8,128)S(1)}) custom-call(s32[16]{0:T(128)S(1)} %reshape_squeeze.3.pos, s32[1]{0:T(128)} %bitcast.6.cnt, f32[512,512]{1,0:T(8,128)S(1)} %copy-done.1, f32[512,512]{1,0:T(8,128)S(1)} %copy-done.3, f32[2,4,256,128]{3,2,1,0:T(8,128)S(1)} %get-tuple-element.12.lower, ...), custom_call_target="tpu_custom_call" | custom-call | tf_op jit(solution)/shard_map/frames/pallas_call | solution.py:551
  49.6 65.4 %combine.1 = (f32[2,4,256,128]{3,2,1,0:T(8,128)S(1)}, f32[2,2,512,128]{3,2,1,0:T(8,128)S(1)}, f32[2048,256]{1,0:T(8,128)S(1)}) custom-call(f32[2,6,768,128]{3,2,1,0:T(8,128)S(1)} %get-tuple-element.15.refs_0_, f32[2048,256]{1,0:T(8,128)S(1)} %bitcast.9), custom_call_target="tpu_custom_call" | custom-call | tf_op jit(solution)/shard_map/combine/pallas_call | solution.py:590
  115.0 3.0 %finish.1 = (f32[512,512]{1,0:T(8,128)}, f32[512,512]{1,0:T(8,128)}, f32[4,256,256]{2,1,0:T(8,128)}, f32[4,256,256]{2,1,0:T(8,128)}) custom-call(f32[2,6,768,128]{3,2,1,0:T(8,128)S(1)} %get-tuple-element.15.refs_0_, f32[2,4,256,128]{3,2,1,0:T(8,128)S(1)} %get-tuple-element.17.refs_1_, f32[2,2,512,128]{3,2,1,0:T(8,128)S(1)} %get-tuple-element.18.refs_2_, ...), custom_call_target="tpu_custom_call" | custom-call | tf_op jit(solution)/shard_map/finish/pallas_call | solution.py:621
Async XLA Ops:
  2.1 1.2 %copy-start = (f32[512,512]{1,0:T(8,128)S(1)}, f32[512,512]{1,0:T(8,128)}, u32[]{:S(2)}) copy-start(f32[512,512]{1,0:T(8,128)} %refs_4_.1) | copy-start | bytes 3145732
  3.3 1.2 %copy-start.2 = (f32[512,512]{1,0:T(8,128)S(1)}, f32[512,512]{1,0:T(8,128)}, u32[]{:S(2)}) copy-start(f32[512,512]{1,0:T(8,128)} %refs_5_.1) | copy-start | bytes 3145732
  4.6 1.6 %copy-start.6 = (f32[1,1,8,256,256]{4,3,2,1,0:T(8,128)S(1)}, f32[1,1,8,256,256]{4,3,2,1,0:T(8,128)}, u32[]{:S(2)}) copy-start(f32[1,1,8,256,256]{4,3,2,1,0:T(8,128)} %param.13) | copy-start | bytes 6291460
  6.2 0.9 copy-start.8
  7.1 29.3 %copy-start.1 = (f32[512,512]{1,0:T(8,128)S(1)}, f32[512,512]{1,0:T(8,128)}, u32[]{:S(2)}) copy-start(f32[512,512]{1,0:T(8,128)} %refs_4_.1) | copy-start | bytes 3145732
  7.1 29.3 %copy-start.3 = (f32[512,512]{1,0:T(8,128)S(1)}, f32[512,512]{1,0:T(8,128)}, u32[]{:S(2)}) copy-start(f32[512,512]{1,0:T(8,128)} %refs_5_.1) | copy-start | bytes 3145732
  7.1 29.3 %copy-start.4 = (f32[4,256,256]{2,1,0:T(8,128)S(1)}, f32[4,256,256]{2,1,0:T(8,128)}, u32[]{:S(2)}) copy-start(f32[4,256,256]{2,1,0:T(8,128)} %refs_6_.1) | copy-start | bytes 3145732
  7.1 29.3 %copy-start.5 = (f32[4,256,256]{2,1,0:T(8,128)S(1)}, f32[4,256,256]{2,1,0:T(8,128)}, u32[]{:S(2)}) copy-start(f32[4,256,256]{2,1,0:T(8,128)} %refs_7_.1) | copy-start | bytes 3145732
  36.4 1.0 copy-start.7

commit v2 on v1

--- a/solution.py
+++ b/solution.py
@@ -20,13 +20,17 @@
 SPAN = TILE + SIZE
 SLOTS = 8
 CHUNK = 32
-VMEM_LIMIT = 56 * 2**20
+HALO_LIMIT = 56 * 2**20
+LOWER = 0
+WIDE = 8
+AMPS = 20
+BLOCKS = 288
 SCHEDULE = (
     ("corner", ("far", 0)),
     (),
-    (("side", 0),),
+    (("far", 1),),
     (),
-    (("far", 1), ("near", 0)),
+    (("near", 0), ("side", 0)),
     (("near", 1), ("side", 1)),
 )
 
@@ -46,12 +50,6 @@
     return np.stack(found)
 
 
-def parity_order():
-    order = np.concatenate([np.arange(0, SIZE, 2), np.arange(1, SIZE, 2)])
-    right = np.arange(SIZE)[:, None] == order[None, :]
-    return np.stack([right, right.T]).astype(BF16)
-
-
 def dot(a, b):
     return jnp.dot(a, b, preferred_element_type=F32)
 
@@ -67,29 +65,35 @@
     pl.semaphore_wait(barrier, len(peers))
 
 
-def halo_kernel(rows, cols, obj_r, obj_i, amp, order, lower, wide, amp_out, send_sem, recv_sem):
+def halo_kernel(
+    rows, cols, obj_r, obj_i, amp_in, mail, amp, sorted_amp, order, load_sem, store_sem, send_sem, recv_sem
+):
     row, col = grid_place()
     up = (lax.rem(row + rows - 1, rows), col)
     down = (lax.rem(row + 1, rows), col)
     left = (row, lax.rem(col + cols - 1, cols))
     right = (row, lax.rem(col + 1, cols))
+    loads = [pltpu.make_async_copy(amp_in.at[s], amp.at[s], load_sem.at[s]) for s in range(SLOTS)]
+    for copy in loads:
+        copy.start()
     greet((up, down, left, right))
     objs = (obj_r, obj_i)
+    has_up, has_down, has_left, has_right = row > 0, row < rows - 1, col > 0, col < cols - 1
 
     def band(part, j, number):
         return pltpu.make_async_remote_copy(
             src_ref=objs[part].at[pl.ds(0, SIZE), pl.ds(j * LANES, LANES)],
-            dst_ref=lower.at[part, j],
+            dst_ref=mail.at[LOWER + part * 4 + j],
             send_sem=send_sem.at[number],
             recv_sem=recv_sem.at[number],
             device_id=up,
             device_id_type=MESH,
         )
 
-    def side(part, j, number):
+    def side(part, j, third, number):
         return pltpu.make_async_remote_copy(
-            src_ref=objs[part].at[:, pl.ds(j * LANES, LANES)],
-            dst_ref=wide.at[part, j, pl.ds(0, TILE), :],
+            src_ref=objs[part].at[pl.ds(third * SIZE, SIZE), pl.ds(j * LANES, LANES)],
+            dst_ref=mail.at[WIDE + (part * 2 + j) * 3 + third],
             send_sem=send_sem.at[number],
             recv_sem=recv_sem.at[number],
             device_id=left,
@@ -98,8 +102,8 @@
 
     def corner(part, j, number):
         return pltpu.make_async_remote_copy(
-            src_ref=lower.at[part, j],
-            dst_ref=wide.at[part, j, pl.ds(TILE, SIZE), :],
+            src_ref=mail.at[LOWER + part * 4 + j],
+            dst_ref=mail.at[WIDE + (part * 2 + j) * 3 + 2],
             send_sem=send_sem.at[number],
             recv_sem=recv_sem.at[number],
             device_id=left,
@@ -107,10 +111,35 @@
         )
 
     bands = [band(part, j, 2 * j + part) for j in range(4) for part in range(2)]
-    sides = [side(part, j, 8 + 2 * j + part) for j in range(2) for part in range(2)]
-    corners = [corner(part, j, 12 + 2 * j + part) for j in range(2) for part in range(2)]
-    for copy in bands + sides:
-        copy.start()
+    sides = [
+        side(part, j, third, 8 + 4 * third + 2 * j + part)
+        for third in range(2)
+        for j in range(2)
+        for part in range(2)
+    ]
+    corners = [corner(part, j, 16 + 2 * j + part) for j in range(2) for part in range(2)]
+
+    @pl.when(has_up)
+    def _():
+        for copy in bands:
+            copy.start()
+
+    @pl.when(has_left)
+    def _():
+        for copy in sides:
+            copy.start()
+
+    half = SIZE // 2
+    first = lax.broadcasted_iota(jnp.int32, (SIZE, SIZE), 0)
+    second = lax.broadcasted_iota(jnp.int32, (SIZE, SIZE), 1)
+
+    def source(i):
+        return jnp.where(i < half, 2 * i, 2 * (i - half) + 1)
+
+    order[0] = jnp.where(first == source(second), 1.0, 0.0).astype(BF16)
+    order[1] = jnp.where(second == source(first), 1.0, 0.0).astype(BF16)
+    for copy in loads:
+        copy.wait()
 
     def sort(slot, carry):
         a = amp[slot]
@@ -124,19 +153,55 @@
             piece = by_row.astype(BF16)
             total += dot(piece, order[0])
             by_row = by_row - piece.astype(F32)
-        amp_out[slot] = total
+        sorted_amp[2 * slot] = total[:, :half]
+        sorted_amp[2 * slot + 1] = total[:, half:]
         return carry
 
     lax.fori_loop(0, SLOTS, sort, 0)
+    store = pltpu.make_async_copy(sorted_amp, mail.at[pl.ds(AMPS, 2 * SLOTS)], store_sem)
+    store.start()
+
     for number in range(4):
-        bands[number].wait_recv()
-        corners[number].start()
-    for copy in bands:
-        copy.wait_send()
-    for copy in bands[4:]:
-        copy.wait_recv()
-    for copy in sides + corners:
-        copy.wait()
+
+        @pl.when(has_down)
+        def _():
+            bands[number].wait_recv()
+
+        @pl.when(has_down & has_left)
+        def _():
+            corners[number].start()
+
+    @pl.when(has_down)
+    def _():
+        for copy in bands[4:]:
+            copy.wait_recv()
+
+    @pl.when(has_up)
+    def _():
+        for copy in bands:
+            copy.wait_send()
+
+    @pl.when(has_right)
+    def _():
+        for copy in sides:
+            copy.wait_recv()
+
+    @pl.when(has_left)
+    def _():
+        for copy in sides:
+            copy.wait_send()
+
+    @pl.when(has_down & has_right)
+    def _():
+        for copy in corners:
+            copy.wait_recv()
+
+    @pl.when(has_down & has_left)
+    def _():
+        for copy in corners:
+            copy.wait_send()
+
+    store.wait()
 
 
 def frames_kernel(
@@ -144,14 +209,14 @@
     cnt,
     obj_r,
     obj_i,
-    lower,
-    wide,
-    amp,
+    mail,
     pr,
     pi,
-    tab,
+    tab_in,
     acc,
     pg,
+    tab,
+    amp,
     ext,
     pat_r,
     pat_i,
@@ -168,9 +233,24 @@
 ):
     half = SIZE // 2
     loads = [
-        pltpu.make_async_copy(lower, ext.at[:, pl.ds(0, 4), pl.ds(TILE, SIZE), :], sem.at[0]),
-        pltpu.make_async_copy(wide, ext.at[:, pl.ds(4, 2)], sem.at[1]),
+        pltpu.make_async_copy(
+            mail.at[pl.ds(LOWER + 4 * part, 4)],
+            ext.at[part, pl.ds(0, 4), pl.ds(TILE, SIZE), :],
+            sem.at[part],
+        )
+        for part in range(2)
+    ] + [
+        pltpu.make_async_copy(
+            mail.at[WIDE + (part * 2 + j) * 3 + third],
+            ext.at[part, 4 + j, pl.ds(third * SIZE, SIZE), :],
+            sem.at[12 + (part * 2 + j) * 3 + third],
+        )
+        for part in range(2)
+        for j in range(2)
+        for third in range(3)
     ]
+    loads.append(pltpu.make_async_copy(mail.at[pl.ds(AMPS, 2 * SLOTS)], amp, sem.at[11]))
+    loads.append(pltpu.make_async_copy(tab_in, tab, sem.at[10]))
     for part, obj in ((0, obj_r), (1, obj_i)):
         for j in range(4):
             loads.append(
@@ -192,8 +272,8 @@
         copy.wait()
 
     def frame(s, carry):
-        y = pos[2 * s]
-        x = pos[2 * s + 1]
+        y = pos[0, 0, s, 0]
+        x = pos[0, 0, s, 1]
         jb = x // LANES
         sh = x % LANES
         back = (LANES - sh) % LANES
@@ -231,14 +311,16 @@
         far_o[...] = dot(xo[...], tab[3]).reshape(MODES, SIZE, SIZE)
         for c in range(0, SIZE, CHUNK):
             rows = slice(c, c + CHUNK)
-            for far, lanes in ((far_e, slice(0, half)), (far_o, slice(half, SIZE))):
+            for side, far in enumerate((far_e, far_o)):
                 total = None
                 for m in range(MODES):
                     f = far[m, rows]
                     f = f * f
                     f = f[:, :half] + f[:, half:]
                     total = f if total is None else total + f
-                inten[rows, lanes] = 1.0 - amp[s, rows, lanes] * lax.rsqrt(jnp.maximum(total, 0.25))
+                inten[rows, side * half : (side + 1) * half] = 1.0 - amp[2 * s + side, rows] * lax.rsqrt(
+                    jnp.maximum(total, 0.25)
+                )
         for m in range(MODES):
             for p, dst in ((0, xp), (1, xq)):
                 for c in range(0, half, CHUNK):
@@ -291,7 +373,7 @@
                 acc[part, jb + 2, pl.ds(y + c, CHUNK), :] += jnp.where(low, b, 0.0)
         return carry
 
-    lax.fori_loop(0, cnt[0], frame, 0)
+    lax.fori_loop(0, cnt[0, 0], frame, 0)
 
 
 def combine_kernel(
@@ -361,6 +443,7 @@
         )
 
     corner_copy = halo(acc.at[:, pl.ds(4, 2), pl.ds(TILE, SIZE), :], corner, 0, right)
+    has_up, has_down, has_left, has_right = row > 0, row < rows - 1, col > 0, col < cols - 1
     moves = {"corner": corner_copy}
     for part in range(2):
         moves["far", part] = halo(
@@ -373,7 +456,10 @@
 
     def begin(stage):
         for name in SCHEDULE[stage]:
-            moves[name].start()
+
+            @pl.when(has_right if name == "corner" or name[0] == "side" else has_down)
+            def _():
+                moves[name].start()
 
     begin(0)
 
@@ -437,10 +523,14 @@
             )
 
     loads[1].wait()
-    corner_copy.wait_recv()
-    for part in range(2):
-        for j in range(2):
-            band[part, j] += corner[part, j]
+
+    @pl.when(has_left)
+    def _():
+        corner_copy.wait_recv()
+        for part in range(2):
+            for j in range(2):
+                band[part, j] += corner[part, j]
+
     begin(2)
 
     bases = []
@@ -504,20 +594,21 @@
     for copy in pending:
         copy.wait_send()
     for name, copy in moves.items():
+        sideways = name == "corner" or name[0] == "side"
         if name != "corner":
-            copy.wait_recv()
-    for copy in moves.values():
-        copy.wait_send()
+            pl.when(has_left if sideways else has_up)(copy.wait_recv)
+        pl.when(has_right if sideways else has_down)(copy.wait_send)
 
 
 def finish_kernel(step, acc, below, side, result, obj_r, obj_i, pr, pi, new_r, new_i, new_pr, new_pi):
-    upper = pl.program_id(0) < 2
+    row, col = grid_place()
+    upper = (pl.program_id(0) < 2) & (row > 0)
     for part, obj, new in ((0, obj_r, new_r), (1, obj_i, new_i)):
         for j in range(4):
             lanes = slice(j * LANES, (j + 1) * LANES)
             total = acc[part, j] + jnp.where(upper, below[part, j], 0.0)
             if j < 2:
-                total += side[part, j]
+                total += jnp.where(col > 0, side[part, j], 0.0)
             new[:, lanes] = obj[:, lanes] - OBJECT_STEP * total
     for part, old, new in ((0, pr, new_pr), (1, pi, new_pi)):
         new[0] = old[0] - step * result[part, 0]
@@ -532,28 +623,34 @@
     extended = jax.ShapeDtypeStruct((2, 6, SPAN, LANES), F32)
     frame_shape = (SIZE, SIZE)
 
-    lower, wide, amp = pl.pallas_call(
+    mail = pl.pallas_call(
         lambda *refs: halo_kernel(rows, cols, *refs),
-        out_shape=(
-            jax.ShapeDtypeStruct((2, 4, SIZE, LANES), F32),
-            jax.ShapeDtypeStruct((2, 2, SPAN, LANES), F32),
-            jax.ShapeDtypeStruct((SLOTS, SIZE, SIZE), F32),
-        ),
-        in_specs=[anywhere, anywhere, vmem, vmem],
-        out_specs=(anywhere, anywhere, vmem),
-        scratch_shapes=[dma((16,)), dma((16,))],
+        out_shape=jax.ShapeDtypeStruct((BLOCKS, SIZE, LANES), F32),
+        in_specs=[anywhere] * 3,
+        out_specs=anywhere,
+        scratch_shapes=[
+            pltpu.VMEM((SLOTS, SIZE, SIZE), F32),
+            pltpu.VMEM((2 * SLOTS, SIZE, LANES), F32),
+            pltpu.VMEM((2, SIZE, SIZE), BF16),
+            dma((SLOTS,)),
+            dma,
+            dma((20,)),
+            dma((20,)),
+        ],
         compiler_params=pltpu.CompilerParams(
-            collective_id=0, has_side_effects=True, vmem_limit_bytes=16 * 2**20
+            collective_id=0, has_side_effects=True, vmem_limit_bytes=HALO_LIMIT
         ),
         name="halo",
-    )(object_real, object_imag, amplitudes[0, 0], jnp.asarray(parity_order()))
+    )(object_real, object_imag, amplitudes[0, 0])
 
     acc, pg = pl.pallas_call(
         frames_kernel,
         out_shape=(extended, jax.ShapeDtypeStruct((2, MODES, SIZE, SIZE), F32)),
-        in_specs=[smem, smem] + [anywhere] * 4 + [vmem] * 4,
+        in_specs=[smem, smem] + [anywhere] * 3 + [vmem] * 2 + [anywhere],
         out_specs=(vmem, vmem),
         scratch_shapes=[
+            pltpu.VMEM((4, SIZE, SIZE), BF16),
+            pltpu.VMEM((2 * SLOTS, SIZE, LANES), F32),
             pltpu.VMEM((2, 6, SPAN, LANES), F32),
             pltpu.VMEM(frame_shape, F32),
             pltpu.VMEM(frame_shape, F32),
@@ -566,18 +663,16 @@
             pltpu.VMEM(frame_shape, F32),
             pltpu.VMEM(frame_shape, F32),
             pltpu.VMEM(frame_shape, F32),
-            dma((10,)),
+            dma((24,)),
         ],
-        compiler_params=pltpu.CompilerParams(vmem_limit_bytes=32 * 2**20),
+        compiler_params=pltpu.CompilerParams(vmem_limit_bytes=28 * 2**20),
         name="frames",
     )(
-        positions[0, 0].reshape(-1),
-        counts.reshape(-1),
+        positions,
+        counts,
         object_real,
         object_imag,
-        lower,
-        wide,
-        amp,
+        mail,
         probe_real,
         probe_imag,
         jnp.asarray(tables()),

time: 118 us -> 104 us (0.88); the launches traced: 118 us -> 102 us
  Pallas kernels: 110 us -> 100 us
  local copies, waits for them, and re-layouts: 6.88 us -> 0.78 us
    pallas_call x1, Pallas kernels: 65.4 us -> 48.5 us  [shards(): pl.pallas_call(lambda *refs: combine_kernel(rows, cols, *refs), out_shape...]
    pallas_call x1, Pallas kernels: 12.1 us -> 20.1 us  [shards(): pl.pallas_call(frames_kernel, out_shape=(extended, jax.ShapeDtypeStruct((...]
    unnamed x19 -> x11, local copies, waits for them, and re-layouts: 6.8 us -> 0.78 us
where the time goes in v2:
time: 104 us; the launch traced here: 102 us
  Pallas kernels  100 us (96%)
  between operations  1.35 us (1%)
    pallas_call x1, Pallas kernels, shards(): pl.pallas_call(lambda *refs: combine_kernel(rows, cols, *refs), out_shape...  48.5 us
    pallas_call x1, Pallas kernels, shards(): pl.pallas_call(lambda *refs: halo_kernel(rows, cols, *refs), out_shape=ja...  28.3 us
    pallas_call x1, Pallas kernels, shards(): pl.pallas_call(frames_kernel, out_shape=(extended, jax.ShapeDtypeStruct((...  20.1 us
    pallas_call x1, Pallas kernels, shards(): pl.pallas_call(lambda *refs: finish_kernel(step, *refs), grid=(4,), out_s...  3.05 us

profile of v2, /device:TPU:1, one launch (start us, length us, event | category | flops | bytes accessed | tf_op | source)
XLA Modules:
  0.0 102.2 jit_solution(12153985216880510497)
XLA Ops:
  1.3 0.8 copy.12.pos
  2.0 0.0 copy-start
  2.0 0.0 copy-start.1
  2.0 0.0 copy-start.2
  2.0 0.0 copy-start.3
  2.0 0.0 copy-start.4
  2.1 28.3 %halo.1.mail = f32[288,256,128]{2,1,0:T(8,128)} custom-call(f32[512,512]{1,0:T(8,128)} %refs_4_.1, f32[512,512]{1,0:T(8,128)} %refs_5_.1, f32[8,256,256]{2,1,0:T(8,128)} %bitcast.5), custom_call_target="tpu_custom_call" | custom-call | tf_op jit(solution)/shard_map/halo/pallas_call | solution.py:626
  30.4 0.0 copy-done
  30.4 0.0 copy-done.1
  30.4 0.0 copy-done.2
  30.4 0.0 copy-done.3
  30.4 0.0 copy-done.4
  30.5 20.1 %frames.1 = (f32[2,6,768,128]{3,2,1,0:T(8,128)S(1)}, f32[2,4,256,256]{3,2,1,0:T(8,128)S(1)}) custom-call(s32[1,1,8,2]{3,2,1,0:T(8,128)S(1)} %copy.12.pos, s32[1,1]{1,0:T(1,128)S(6)} %copy.13.cnt, f32[512,512]{1,0:T(8,128)S(1)} %copy-done, f32[512,512]{1,0:T(8,128)S(1)} %copy-done.1, f32[288,256,128]{2,1,0:T(8,128)} %halo.1.mail, ...), custom_call_target="tpu_custom_call" | custom-call | tf_op jit(solution)/shard_map/frames/pallas_call | solution.py:646
  50.6 48.5 %combine.1 = (f32[2,4,256,128]{3,2,1,0:T(8,128)S(1)}, f32[2,2,512,128]{3,2,1,0:T(8,128)S(1)}, f32[2048,256]{1,0:T(8,128)S(1)}) custom-call(f32[2,6,768,128]{3,2,1,0:T(8,128)S(1)} %get-tuple-element.9.refs_0_, f32[2048,256]{1,0:T(8,128)S(1)} %bitcast.4), custom_call_target="tpu_custom_call" | custom-call | tf_op jit(solution)/shard_map/combine/pallas_call | solution.py:685
  99.1 3.1 %finish.1 = (f32[512,512]{1,0:T(8,128)}, f32[512,512]{1,0:T(8,128)}, f32[4,256,256]{2,1,0:T(8,128)}, f32[4,256,256]{2,1,0:T(8,128)}) custom-call(f32[2,6,768,128]{3,2,1,0:T(8,128)S(1)} %get-tuple-element.9.refs_0_, f32[2,4,256,128]{3,2,1,0:T(8,128)S(1)} %get-tuple-element.11.refs_1_, f32[2,2,512,128]{3,2,1,0:T(8,128)S(1)} %get-tuple-element.12.refs_2_, ...), custom_call_target="tpu_custom_call" | custom-call | tf_op jit(solution)/shard_map/finish/pallas_call | solution.py:716
Async XLA Ops:
  2.0 28.4 %copy-start = (f32[512,512]{1,0:T(8,128)S(1)}, f32[512,512]{1,0:T(8,128)}, u32[]{:S(2)}) copy-start(f32[512,512]{1,0:T(8,128)} %refs_4_.1) | copy-start | bytes 3145732
  2.0 28.4 %copy-start.1 = (f32[512,512]{1,0:T(8,128)S(1)}, f32[512,512]{1,0:T(8,128)}, u32[]{:S(2)}) copy-start(f32[512,512]{1,0:T(8,128)} %refs_5_.1) | copy-start | bytes 3145732
  2.0 28.4 %copy-start.2 = (f32[4,256,256]{2,1,0:T(8,128)S(1)}, f32[4,256,256]{2,1,0:T(8,128)}, u32[]{:S(2)}) copy-start(f32[4,256,256]{2,1,0:T(8,128)} %refs_6_.1) | copy-start | bytes 3145732
  2.0 28.4 %copy-start.3 = (f32[4,256,256]{2,1,0:T(8,128)S(1)}, f32[4,256,256]{2,1,0:T(8,128)}, u32[]{:S(2)}) copy-start(f32[4,256,256]{2,1,0:T(8,128)} %refs_7_.1) | copy-start | bytes 3145732
  2.0 28.4 %copy-start.4 = (bf16[4,256,256]{2,1,0:T(8,128)(2,1)S(1)}, bf16[4,256,256]{2,1,0:T(8,128)(2,1)}, u32[]{:S(2)}) copy-start(bf16[4,256,256]{2,1,0:T(8,128)(2,1)} %constant.2.clone.tab_in) | copy-start | bytes 1572868

commit v3 on v2

--- a/solution.py
+++ b/solution.py
@@ -19,19 +19,27 @@
 TILE = 512
 SPAN = TILE + SIZE
 SLOTS = 8
+OWN_ROWS = MODES * SIZE
 CHUNK = 32
 HALO_LIMIT = 56 * 2**20
 LOWER = 0
 WIDE = 8
 AMPS = 20
+RELAY = 40
 BLOCKS = 288
+DETOUR = 128
+HOP_ROWS = 64
+EARLY_SIDES = 8
+BAND_STEP = 0
+SIDE_STEP = 0
+CORNER_STEP = 1
 SCHEDULE = (
     ("corner", ("far", 0)),
     (),
     (("far", 1),),
-    (),
-    (("near", 0), ("side", 0)),
-    (("near", 1), ("side", 1)),
+    (("side", 0), ("side", 1)),
+    (("near", 0),),
+    (("near", 1),),
 )
 
 
@@ -76,14 +84,21 @@
     loads = [pltpu.make_async_copy(amp_in.at[s], amp.at[s], load_sem.at[s]) for s in range(SLOTS)]
     for copy in loads:
         copy.start()
-    greet((up, down, left, right))
+    n = 4
+    z, y = lax.rem(row, n), row // n
+    following = (y * n + lax.rem(z + 1, n), col)
+    previous = (y * n + lax.rem(z + n - 1, n), col)
+    y_up = (lax.rem(y + n - 1, n) * n + z, col)
+    y_down = (lax.rem(y + 1, n) * n + z, col)
+    greet((up, down, left, right, following, previous, y_up, y_down))
     objs = (obj_r, obj_i)
     has_up, has_down, has_left, has_right = row > 0, row < rows - 1, col > 0, col < cols - 1
 
     def band(part, j, number):
+        taken = SIZE if j < 3 else SIZE - DETOUR
         return pltpu.make_async_remote_copy(
-            src_ref=objs[part].at[pl.ds(0, SIZE), pl.ds(j * LANES, LANES)],
-            dst_ref=mail.at[LOWER + part * 4 + j],
+            src_ref=objs[part].at[pl.ds(0, taken), pl.ds(j * LANES, LANES)],
+            dst_ref=mail.at[LOWER + part * 4 + j, pl.ds(0, taken), :],
             send_sem=send_sem.at[number],
             recv_sem=recv_sem.at[number],
             device_id=up,
@@ -119,15 +134,43 @@
     ]
     corners = [corner(part, j, 16 + 2 * j + part) for j in range(2) for part in range(2)]
 
-    @pl.when(has_up)
-    def _():
-        for copy in bands:
+    def hop(number, chunk, part):
+        rows_here = pl.ds(SIZE - DETOUR + chunk * HOP_ROWS, HOP_ROWS)
+        place = 20 + (number * (DETOUR // HOP_ROWS) + chunk) * 2 + part
+        if number == 0:
+            src = objs[part].at[rows_here, pl.ds(3 * LANES, LANES)]
+        else:
+            src = mail.at[RELAY + 2 * (number - 1) + part, rows_here, :]
+        return pltpu.make_async_remote_copy(
+            src_ref=src,
+            dst_ref=mail.at[RELAY + 2 * number + part, rows_here, :],
+            send_sem=send_sem.at[place],
+            recv_sem=recv_sem.at[place],
+            device_id=following if number < 3 else y_up,
+            device_id_type=MESH,
+        )
+
+    chunks = DETOUR // HOP_ROWS
+    hops = [[[hop(k, c, part) for part in range(2)] for c in range(chunks)] for k in range(4)]
+    for c in range(chunks):
+        for copy in hops[0][c]:
             copy.start()
-
-    @pl.when(has_left)
-    def _():
-        for copy in sides:
-            copy.start()
+    gives, takes = (z == n - 1) & (y > 0), (z == n - 1) & (y < n - 1)
+
+    def start_bands(group):
+        @pl.when(has_up)
+        def _():
+            for copy in group:
+                copy.start()
+
+    def start_sides(group):
+        @pl.when(has_left)
+        def _():
+            for copy in group:
+                copy.start()
+
+    start_bands(bands[:4])
+    start_sides(sides[:EARLY_SIDES])
 
     half = SIZE // 2
     first = lax.broadcasted_iota(jnp.int32, (SIZE, SIZE), 0)
@@ -161,15 +204,33 @@
     store = pltpu.make_async_copy(sorted_amp, mail.at[pl.ds(AMPS, 2 * SLOTS)], store_sem)
     store.start()
 
-    for number in range(4):
-
-        @pl.when(has_down)
-        def _():
-            bands[number].wait_recv()
-
-        @pl.when(has_down & has_left)
-        def _():
-            corners[number].start()
+    def start_corners():
+        for number in range(4):
+
+            @pl.when(has_down)
+            def _():
+                bands[number].wait_recv()
+
+            @pl.when(has_down & has_left)
+            def _():
+                corners[number].start()
+
+    for step in range(chunks + 2):
+        for k in (2, 1, 0):
+            c = step - k
+            if 0 <= c < chunks:
+                for part in range(2):
+                    hops[k][c][part].wait_recv()
+                    if k < 2:
+                        hops[k + 1][c][part].start()
+                    else:
+                        pl.when(gives)(hops[3][c][part].start)
+        if step == BAND_STEP:
+            start_bands(bands[4:])
+        if step == SIDE_STEP:
+            start_sides(sides[EARLY_SIDES:])
+        if step == CORNER_STEP:
+            start_corners()
 
     @pl.when(has_down)
     def _():
@@ -201,6 +262,12 @@
         for copy in corners:
             copy.wait_send()
 
+    for c in range(chunks):
+        for part in range(2):
+            for k in range(3):
+                hops[k][c][part].wait_send()
+            pl.when(gives)(hops[3][c][part].wait_send)
+            pl.when(takes)(hops[3][c][part].wait_recv)
     store.wait()
 
 
@@ -231,12 +298,28 @@
     og_i,
     sem,
 ):
+    row, col = grid_place()
+    arrived = jnp.where(lax.rem(row, 4) == 3, 2, 0)
     half = SIZE // 2
     loads = [
         pltpu.make_async_copy(
-            mail.at[pl.ds(LOWER + 4 * part, 4)],
-            ext.at[part, pl.ds(0, 4), pl.ds(TILE, SIZE), :],
+            mail.at[pl.ds(LOWER + 4 * part, 3)],
+            ext.at[part, pl.ds(0, 3), pl.ds(TILE, SIZE), :],
             sem.at[part],
+        )
+        for part in range(2)
+    ] + [
+        pltpu.make_async_copy(
+            mail.at[LOWER + 4 * part + 3, pl.ds(0, SIZE - DETOUR), :],
+            ext.at[part, 3, pl.ds(TILE, SIZE - DETOUR), :],
+            sem.at[24 + part],
+        )
+        for part in range(2)
+    ] + [
+        pltpu.make_async_copy(
+            mail.at[RELAY + 4 + arrived + part, pl.ds(SIZE - DETOUR, DETOUR), :],
+            ext.at[part, 3, pl.ds(TILE + SIZE - DETOUR, DETOUR), :],
+            sem.at[26 + part],
         )
         for part in range(2)
     ] + [
@@ -251,17 +334,11 @@
     ]
     loads.append(pltpu.make_async_copy(mail.at[pl.ds(AMPS, 2 * SLOTS)], amp, sem.at[11]))
     loads.append(pltpu.make_async_copy(tab_in, tab, sem.at[10]))
+    for copy in loads:
+        copy.start()
     for part, obj in ((0, obj_r), (1, obj_i)):
         for j in range(4):
-            loads.append(
-                pltpu.make_async_copy(
-                    obj.at[:, pl.ds(j * LANES, LANES)],
-                    ext.at[part, j, pl.ds(0, TILE), :],
-                    sem.at[2 + 4 * part + j],
-                )
-            )
-    for copy in loads:
-        copy.start()
+            ext[part, j, :TILE] = obj[:, j * LANES : (j + 1) * LANES]
     blank = jnp.zeros((SPAN, LANES), F32)
     for part in range(2):
         for j in range(6):
@@ -419,7 +496,9 @@
     plane_at = (x, y)
 
     loads = [
-        pltpu.make_async_copy(pg, data, local_sem.at[0]),
+        pltpu.make_async_copy(
+            pg.at[pl.ds(pl.multiple_of(core * OWN_ROWS, OWN_ROWS), OWN_ROWS), :], data, local_sem.at[0]
+        ),
         pltpu.make_async_copy(
             acc.at[:, pl.ds(0, 2), pl.ds(TILE, SIZE), :], band, local_sem.at[1]
         ),
@@ -461,8 +540,6 @@
             def _():
                 moves[name].start()
 
-    begin(0)
-
     numbers = iter(range(82))
     pending = []
 
@@ -490,21 +567,22 @@
     piece = quarter // (n * n)
     mine = core * kept
     theirs = (1 - core) * kept
-    loads[0].wait()
     core_copies = [
         send(
-            data.at[aligned(theirs + part * part_rows, part_rows), :],
+            pg.at[aligned(theirs + part * part_rows, part_rows), :],
             rbuf0.at[pl.ds(part * part_rows, part_rows), :],
             other,
         )
         for part in range(2)
     ]
 
+    begin(0)
     begin(1)
+    loads[0].wait()
     line_copies = []
     for part in range(2):
         core_copies[part].wait_recv()
-        base = mine + part * part_rows
+        base = part * part_rows
 
         def add_core(i, carry, base=base, part=part):
             here = aligned(base + i * quarter, quarter)
@@ -538,7 +616,7 @@
     for part in range(2):
         for k in range(3):
             line_copies[part * 3 + k].wait_recv()
-        base = mine + part * part_rows + line_at[part] * quarter
+        base = part * part_rows + line_at[part] * quarter
         bases.append(base)
         here = aligned(base, quarter)
         total = data[here, :]
@@ -560,8 +638,9 @@
     for part in range(2):
         for k in range(15):
             plane_copies[part * 15 + k].wait_recv()
-        here = aligned(bases[part] + (plane_at[part] * n + z) * piece, piece)
-        total = data[here, :]
+        offset = bases[part] + (plane_at[part] * n + z) * piece
+        total = data[aligned(offset, piece), :]
+        here = aligned(mine + offset, piece)
         for k in range(15):
             total += rbuf2[(part * 15 + k) * piece : (part * 15 + k + 1) * piece, :]
         result[here, :] = total
@@ -575,12 +654,12 @@
     for part in range(2):
         for k in range(15):
             gather_copies[part * 15 + k].wait_recv()
-        here = result.at[aligned(bases[part], quarter), :]
+        here = result.at[aligned(mine + bases[part], quarter), :]
         for k in (1, 2, 3):
             line_copies.append(send(here, here, lines[part][k - 1]))
     core_copies = []
     for part in range(2):
-        here = result.at[aligned(bases[part], quarter), :]
+        here = result.at[aligned(mine + bases[part], quarter), :]
         core_copies.append(send(here, here, other))
     begin(5)
     for k in (1, 3, 2):
@@ -602,7 +681,7 @@
 
 def finish_kernel(step, acc, below, side, result, obj_r, obj_i, pr, pi, new_r, new_i, new_pr, new_pi):
     row, col = grid_place()
-    upper = (pl.program_id(0) < 2) & (row > 0)
+    upper = (pl.program_id(0) < 1) & (row > 0)
     for part, obj, new in ((0, obj_r, new_r), (1, obj_i, new_i)):
         for j in range(4):
             lanes = slice(j * LANES, (j + 1) * LANES)
@@ -611,7 +690,7 @@
                 total += jnp.where(col > 0, side[part, j], 0.0)
             new[:, lanes] = obj[:, lanes] - OBJECT_STEP * total
     for part, old, new in ((0, pr, new_pr), (1, pi, new_pi)):
-        new[0] = old[0] - step * result[part, 0]
+        new[...] = old[...] - step * result[part]
 
 
 def shards(object_real, object_imag, probe_real, probe_imag, amplitudes, positions, counts):
@@ -634,8 +713,8 @@
             pltpu.VMEM((2, SIZE, SIZE), BF16),
             dma((SLOTS,)),
             dma,
-            dma((20,)),
-            dma((20,)),
+            dma((20 + 8 * (DETOUR // HOP_ROWS),)),
+            dma((20 + 8 * (DETOUR // HOP_ROWS),)),
         ],
         compiler_params=pltpu.CompilerParams(
             collective_id=0, has_side_effects=True, vmem_limit_bytes=HALO_LIMIT
@@ -646,7 +725,7 @@
     acc, pg = pl.pallas_call(
         frames_kernel,
         out_shape=(extended, jax.ShapeDtypeStruct((2, MODES, SIZE, SIZE), F32)),
-        in_specs=[smem, smem] + [anywhere] * 3 + [vmem] * 2 + [anywhere],
+        in_specs=[smem, smem] + [vmem] * 2 + [anywhere] + [vmem] * 2 + [anywhere],
         out_specs=(vmem, vmem),
         scratch_shapes=[
             pltpu.VMEM((4, SIZE, SIZE), BF16),
@@ -663,7 +742,7 @@
             pltpu.VMEM(frame_shape, F32),
             pltpu.VMEM(frame_shape, F32),
             pltpu.VMEM(frame_shape, F32),
-            dma((24,)),
+            dma((28,)),
         ],
         compiler_params=pltpu.CompilerParams(vmem_limit_bytes=28 * 2**20),
         name="frames",
@@ -694,7 +773,7 @@
         scratch_shapes=[
             pltpu.VMEM((2, 2, SIZE, LANES), F32),
             pltpu.VMEM((2, 2, SIZE, LANES), F32),
-            pltpu.VMEM((whole, SIZE), F32),
+            pltpu.VMEM((whole // 2, SIZE), F32),
             pltpu.VMEM((whole // 2, SIZE), F32),
             pltpu.VMEM((whole // 2 * 3 // 4, SIZE), F32),
             pltpu.VMEM((30 * whole // 256, SIZE), F32),
@@ -710,18 +789,18 @@
         name="combine",
     )(acc, pg.reshape(whole, SIZE))
 
-    part = TILE // 4
+    part = TILE // 2
     tile_block = pl.BlockSpec((part, TILE), lambda i: (i, 0))
-    probe_block = pl.BlockSpec((1, SIZE, SIZE), lambda i: (i, 0, 0))
+    probe_block = pl.BlockSpec((2, SIZE, SIZE), lambda i: (i, 0, 0))
     return pl.pallas_call(
         lambda *refs: finish_kernel(step, *refs),
-        grid=(4,),
+        grid=(2,),
         out_shape=(tile_shape, tile_shape, probe_shape, probe_shape),
         in_specs=[
             pl.BlockSpec((2, 4, part, LANES), lambda i: (0, 0, i, 0)),
-            pl.BlockSpec((2, 4, part, LANES), lambda i: (0, 0, jnp.minimum(i, 1), 0)),
+            pl.BlockSpec((2, 4, SIZE, LANES), lambda i: (0, 0, 0, 0)),
             pl.BlockSpec((2, 2, part, LANES), lambda i: (0, 0, i, 0)),
-            pl.BlockSpec((2, 1, SIZE, SIZE), lambda i: (0, i, 0, 0)),
+            pl.BlockSpec((2, 2, SIZE, SIZE), lambda i: (0, i, 0, 0)),
             tile_block,
             tile_block,
             probe_block,

time: 104 us -> 102 us (0.981)
  the two profiles are of different devices: /device:TPU:1 before, /device:TPU:9 now
where the time goes in v3:
time: 102 us; the launch traced here: 103 us
  Pallas kernels  101 us (99%)
  between operations  1.35 us (1%)
    pallas_call x1, Pallas kernels, shards(): pl.pallas_call(lambda *refs: combine_kernel(rows, cols, *refs), out_shape...  49.9 us
    pallas_call x1, Pallas kernels, shards(): pl.pallas_call(lambda *refs: halo_kernel(rows, cols, *refs), out_shape=ja...  25.4 us
    pallas_call x1, Pallas kernels, shards(): pl.pallas_call(frames_kernel, out_shape=(extended, jax.ShapeDtypeStruct((...  22.6 us
    pallas_call x1, Pallas kernels, shards(): pl.pallas_call(lambda *refs: finish_kernel(step, *refs), grid=(2,), out_s...  2.76 us

profile of v3, /device:TPU:9, one launch (start us, length us, event | category | flops | bytes accessed | tf_op | source)
XLA Modules:
  0.0 102.8 jit_solution(5895970567112427212)
XLA Ops:
  1.3 0.8 copy.12.pos
  2.0 0.0 copy-start
  2.0 0.0 copy-start.1
  2.0 0.0 copy-start.2
  2.0 0.0 copy-start.3
  2.0 0.0 copy-start.4
  2.1 25.4 %halo.1.mail = f32[288,256,128]{2,1,0:T(8,128)} custom-call(f32[512,512]{1,0:T(8,128)} %refs_4_.1, f32[512,512]{1,0:T(8,128)} %refs_5_.1, f32[8,256,256]{2,1,0:T(8,128)} %bitcast.5), custom_call_target="tpu_custom_call" | custom-call | tf_op jit(solution)/shard_map/halo/pallas_call | solution.py:705
  27.5 0.0 copy-done
  27.5 0.0 copy-done.1
  27.5 0.0 copy-done.2
  27.5 0.0 copy-done.3
  27.5 0.0 copy-done.4
  27.6 22.6 %frames.1 = (f32[2,6,768,128]{3,2,1,0:T(8,128)S(1)}, f32[2,4,256,256]{3,2,1,0:T(8,128)S(1)}) custom-call(s32[1,1,8,2]{3,2,1,0:T(8,128)S(1)} %copy.12.pos, s32[1,1]{1,0:T(1,128)S(6)} %copy.13.cnt, f32[512,512]{1,0:T(8,128)S(1)} %copy-done, f32[512,512]{1,0:T(8,128)S(1)} %copy-done.1, f32[288,256,128]{2,1,0:T(8,128)} %halo.1.mail, ...), custom_call_target="tpu_custom_call" | custom-call | tf_op jit(solution)/shard_map/frames/pallas_call | solution.py:725
  50.1 49.9 %combine.1 = (f32[2,4,256,128]{3,2,1,0:T(8,128)S(1)}, f32[2,2,512,128]{3,2,1,0:T(8,128)S(1)}, f32[2048,256]{1,0:T(8,128)S(1)}) custom-call(f32[2,6,768,128]{3,2,1,0:T(8,128)S(1)} %get-tuple-element.9.refs_0_, f32[2048,256]{1,0:T(8,128)S(1)} %bitcast.4), custom_call_target="tpu_custom_call" | custom-call | tf_op jit(solution)/shard_map/combine/pallas_call | solution.py:764
  100.0 2.8 %finish.1 = (f32[512,512]{1,0:T(8,128)}, f32[512,512]{1,0:T(8,128)}, f32[4,256,256]{2,1,0:T(8,128)}, f32[4,256,256]{2,1,0:T(8,128)}) custom-call(f32[2,6,768,128]{3,2,1,0:T(8,128)S(1)} %get-tuple-element.9.refs_0_, f32[2,4,256,128]{3,2,1,0:T(8,128)S(1)} %get-tuple-element.11.refs_1_, f32[2,2,512,128]{3,2,1,0:T(8,128)S(1)} %get-tuple-element.12.refs_2_, ...), custom_call_target="tpu_custom_call" | custom-call | tf_op jit(solution)/shard_map/finish/pallas_call | solution.py:795
Async XLA Ops:
  2.0 25.5 %copy-start = (f32[512,512]{1,0:T(8,128)S(1)}, f32[512,512]{1,0:T(8,128)}, u32[]{:S(2)}) copy-start(f32[512,512]{1,0:T(8,128)} %refs_4_.1) | copy-start | bytes 3145732
  2.0 25.5 %copy-start.1 = (f32[512,512]{1,0:T(8,128)S(1)}, f32[512,512]{1,0:T(8,128)}, u32[]{:S(2)}) copy-start(f32[512,512]{1,0:T(8,128)} %refs_5_.1) | copy-start | bytes 3145732
  2.0 25.5 %copy-start.2 = (f32[4,256,256]{2,1,0:T(8,128)S(1)}, f32[4,256,256]{2,1,0:T(8,128)}, u32[]{:S(2)}) copy-start(f32[4,256,256]{2,1,0:T(8,128)} %refs_6_.1) | copy-start | bytes 3145732
  2.0 25.5 %copy-start.3 = (f32[4,256,256]{2,1,0:T(8,128)S(1)}, f32[4,256,256]{2,1,0:T(8,128)}, u32[]{:S(2)}) copy-start(f32[4,256,256]{2,1,0:T(8,128)} %refs_7_.1) | copy-start | bytes 3145732
  2.0 25.5 %copy-start.4 = (bf16[4,256,256]{2,1,0:T(8,128)(2,1)S(1)}, bf16[4,256,256]{2,1,0:T(8,128)(2,1)}, u32[]{:S(2)}) copy-start(bf16[4,256,256]{2,1,0:T(8,128)(2,1)} %constant.2.clone.tab_in) | copy-start | bytes 1572868
